TPU v7x, 512 devices: a whole 4x4x16 slice. The times are simulated.
512 devices in a mesh: tm: 32 (over z_lo, x, core), space: 16 (over y, z_hi).
Axes of the slice: x: 4, y: 4, z: 16 (z_hi: 4, z_lo: 4; z = z_hi * 4 + z_lo), core: 2. Of those that a mesh axis runs over, the one named last changes fastest.
Arguments:
- queries: bfloat16 [32, 256, 8, 512], P('tm', 'space'), may hold values from -6 to 6
- key_vectors: bfloat16 [32, 256, 8, 512], P('tm', 'space'), may hold values from -6 to 6
- values: bfloat16 [32, 256, 8, 512], P('tm', 'space'), may hold values from -6 to 6
- cotangent: bfloat16 [32, 256, 8, 512], P('tm', 'space'), may hold values from -6 to 6
- dilation: int32 [8], replicated, may hold values from 1 to 4, as said below
Outputs:
- attended: bfloat16 [32, 256, 8, 512], P('tm', 'space')
- grad_queries: bfloat16 [32, 256, 8, 512], P('tm', 'space')
- grad_keys: bfloat16 [32, 256, 8, 512], P('tm', 'space')
- grad_values: bfloat16 [32, 256, 8, 512], P('tm', 'space')
Inputs may be any that keep to these rules, and one draw needn't show every extreme that they name: Exactly 2 heads have dilation 1, 2 have dilation 2 and the others 4; which heads is drawn.
All inputs are finite; a program needn't handle non-finite values.
Results may differ from a plain program's by a relative error of at most 0.034.
Values may be sent and summed in bfloat16 or wider, within the bound.
A program may use at most 128 MiB of HBM per device.

v0:
```python
import jax
import jax.numpy as jnp
from jax import lax
from jax.sharding import PartitionSpec as P

HEAD_DIM = 64
KERNEL = 7


def passed_along(value, axis, steps):
    count = lax.axis_size(axis)
    initial, last = (max(0, -steps), min(count, count - steps))
    return lax.ppermute(value, axis, [(source, source + steps) for source in range(initial, last)])


def neighbour_mask(
    frame_count,
    rows_in,
    cols_in,
    frame_reach,
    step,
    frame_start,
    row_start,
    total_frames,
    total_rows,
):
    frame_query = jnp.arange(frame_count, dtype=jnp.int32)[:, None]
    frame_key = jnp.arange(frame_count + 2 * frame_reach, dtype=jnp.int32)[None, :]
    frame_global = frame_start + frame_key - frame_reach
    frame_ok = (
        (jnp.abs(frame_key - frame_reach - frame_query) <= frame_reach)
        & (frame_global >= 0)
        & (frame_global < total_frames)
    )
    row_query = jnp.arange(rows_in, dtype=jnp.int32)[None, :, None]
    row_key = jnp.arange(rows_in + 2 * frame_reach, dtype=jnp.int32)[None, None, :]
    residues = jnp.arange(step, dtype=jnp.int32)[:, None, None]
    row_global = row_start + (row_key - frame_reach) * step + residues
    row_ok = (
        (jnp.abs(row_key - frame_reach - row_query) <= frame_reach)
        & (row_global >= 0)
        & (row_global < total_rows)
    )
    col_query = jnp.arange(cols_in, dtype=jnp.int32)[:, None]
    col_key = jnp.arange(cols_in, dtype=jnp.int32)[None, :]
    col_ok = jnp.abs(col_key - col_query) <= frame_reach
    allowed = (
        frame_ok[None, :, None, None, :, None, None]
        & row_ok[:, None, :, None, None, :, None]
        & col_ok[None, None, None, :, None, None, :]
    )
    key_count = (frame_count + 2 * frame_reach) * (rows_in + 2 * frame_reach) * cols_in
    return allowed.reshape(step, frame_count * rows_in * cols_in, key_count)


def masked_scores(query_block, key_block, allowed):
    scores = jnp.einsum(
        "abqhe,abkhe->abhqk", query_block, key_block, preferred_element_type=jnp.float32
    ) * HEAD_DIM ** (-0.5)
    return jnp.where(allowed[:, None, None], scores, -1e30)


def frame_move(portion, offset):
    return passed_along(portion, "tm", offset)


def row_move(portion, offset):
    return passed_along(portion, "space", offset)


def frame_back(portion, offset):
    return passed_along(portion, "tm", offset)


def row_back(portion, offset):
    return passed_along(portion, "space", offset)


def extend(stacked, axis_dim, reach, mover):
    length_in = stacked.shape[axis_dim]
    hop_count = -(-reach // length_in)
    lower_parts = []
    upper_parts = []
    for distance in range(1, hop_count + 1):
        amount = min(length_in, reach - (distance - 1) * length_in)
        lower_parts.insert(
            0,
            mover(
                lax.slice_in_dim(stacked, length_in - amount, length_in, axis=axis_dim), distance
            ),
        )
        upper_parts.append(mover(lax.slice_in_dim(stacked, 0, amount, axis=axis_dim), -distance))
    return jnp.concatenate(lower_parts + [stacked] + upper_parts, axis=axis_dim)


def add_part(middle, axis_dim, start, portion):
    current = lax.slice_in_dim(middle, start, start + portion.shape[axis_dim], axis=axis_dim)
    return lax.dynamic_update_slice_in_dim(middle, current + portion, start, axis=axis_dim)


def retract(partial_sum, axis_dim, reach, length_in, mover):
    middle = lax.slice_in_dim(partial_sum, reach, reach + length_in, axis=axis_dim)
    hop_count = -(-reach // length_in)
    low_edge = reach
    high_edge = reach + length_in
    for distance in range(1, hop_count + 1):
        amount = min(length_in, reach - (distance - 1) * length_in)
        lower_part = lax.slice_in_dim(partial_sum, low_edge - amount, low_edge, axis=axis_dim)
        upper_part = lax.slice_in_dim(partial_sum, high_edge, high_edge + amount, axis=axis_dim)
        low_edge = low_edge - amount
        high_edge = high_edge + amount
        middle = add_part(middle, axis_dim, length_in - amount, mover(lower_part, -distance))
        middle = add_part(middle, axis_dim, 0, mover(upper_part, distance))
    return middle


def to_classes(array, step):
    frames, rows, cols, group_size, head_size = array.shape
    shaped = array.reshape(frames, rows // step, step, cols // step, step, group_size, head_size)
    shaped = jnp.transpose(shaped, (2, 4, 0, 1, 3, 5, 6))
    return shaped.reshape(step, step, -1, group_size, head_size)


def from_classes(array, step, frames, rows, cols):
    group_size, head_size = (array.shape[-2], array.shape[-1])
    shaped = array.reshape(step, step, frames, rows // step, cols // step, group_size, head_size)
    shaped = jnp.transpose(shaped, (2, 3, 0, 4, 1, 5, 6))
    return shaped.reshape(frames, rows, cols, group_size, head_size)


def shards(queries, key_vectors, values, cotangent, dilation):
    frame_count, row_count, col_count, width = queries.shape
    head_count = dilation.shape[0]
    head_size = width // head_count
    head_order = jnp.argsort(dilation, stable=True)
    head_restore = jnp.argsort(head_order, stable=True)

    def sort_heads(array, permutation):
        return jnp.take(
            array.reshape(frame_count, row_count, col_count, head_count, head_size),
            permutation,
            axis=3,
        )

    sorted_query = sort_heads(queries, head_order)
    sorted_grad = sort_heads(cotangent, head_order)
    stacked = jnp.stack([sort_heads(key_vectors, head_order), sort_heads(values, head_order)], 0)
    frame_start = lax.axis_index("tm") * frame_count
    row_start = lax.axis_index("space") * row_count
    total_frames = frame_count * lax.axis_size("tm")
    total_rows = row_count * lax.axis_size("space")
    frame_reach = KERNEL // 2
    quarter = head_count // 4
    groups = ((1, 0, quarter), (2, quarter, quarter), (4, 2 * quarter, head_count - 2 * quarter))
    framed = extend(stacked, 1, frame_reach, frame_move)
    records = []
    attended_parts = []
    for dilation_step, first_head, group_size in groups:
        row_reach = frame_reach * dilation_step
        tile = extend(framed[..., first_head : first_head + group_size, :], 2, row_reach, row_move)
        key_frames, key_rows = (tile.shape[1], tile.shape[2])
        class_rows = key_rows // dilation_step
        class_cols = col_count // dilation_step
        tile_classes = tile.reshape(
            2,
            key_frames,
            class_rows,
            dilation_step,
            class_cols,
            dilation_step,
            group_size,
            head_size,
        )
        tile_classes = jnp.transpose(tile_classes, (0, 3, 5, 1, 2, 4, 6, 7)).reshape(
            2, dilation_step, dilation_step, -1, group_size, head_size
        )
        key_block = tile_classes[0]
        value_block = tile_classes[1]
        allowed = neighbour_mask(
            frame_count,
            row_count // dilation_step,
            class_cols,
            frame_reach,
            dilation_step,
            frame_start,
            row_start,
            total_frames,
            total_rows,
        )
        query_block = to_classes(
            sorted_query[..., first_head : first_head + group_size, :], dilation_step
        )
        scores = masked_scores(query_block, key_block, allowed)
        row_peak = jnp.max(scores, axis=-1, keepdims=True)
        row_total = jnp.sum(jnp.exp(scores - row_peak), axis=-1, keepdims=True)
        weights = jnp.exp(scores - row_peak) / row_total
        weights_low = weights.astype(jnp.bfloat16)
        attended_block = jnp.einsum(
            "abhqk,abkhe->abqhe", weights_low, value_block, preferred_element_type=jnp.float32
        ).astype(jnp.bfloat16)
        saved = (row_peak, row_total)
        attended_parts.append(
            from_classes(attended_block, dilation_step, frame_count, row_count, col_count)
        )
        records.append(
            (
                query_block,
                key_block,
                value_block,
                attended_block,
                saved,
                allowed,
                tile.shape,
                key_frames,
                class_rows,
                class_cols,
            )
        )
    grad_query_parts = []
    returned_parts = []
    for group_number in range(len(groups)):
        dilation_step, first_head, group_size = groups[group_number]
        row_reach = frame_reach * dilation_step
        (
            query_block,
            key_block,
            value_block,
            attended_block,
            saved,
            allowed,
            tile_shape,
            key_frames,
            class_rows,
            class_cols,
        ) = records[group_number]
        scores = masked_scores(query_block, key_block, allowed)
        weights = jnp.exp(scores - saved[0]) / saved[1]
        weights_low = weights.astype(jnp.bfloat16)
        grad_block = to_classes(
            sorted_grad[..., first_head : first_head + group_size, :], dilation_step
        )
        delta = jnp.sum(
            grad_block.astype(jnp.float32) * attended_block.astype(jnp.float32), axis=-1
        )
        grad_weights = jnp.einsum(
            "abqhe,abkhe->abhqk", grad_block, value_block, preferred_element_type=jnp.float32
        )
        grad_scores = (
            weights * (grad_weights - jnp.transpose(delta, (0, 1, 3, 2))[..., None])
        ).astype(jnp.bfloat16)
        grad_query_block = jnp.einsum(
            "abhqk,abkhe->abqhe", grad_scores, key_block, preferred_element_type=jnp.float32
        ) * HEAD_DIM ** (-0.5)
        grad_key_block = jnp.einsum(
            "abhqk,abqhe->abkhe", grad_scores, query_block, preferred_element_type=jnp.float32
        ) * HEAD_DIM ** (-0.5)
        grad_value_block = jnp.einsum(
            "abhqk,abqhe->abkhe", weights_low, grad_block, preferred_element_type=jnp.float32
        )
        grad_query_parts.append(
            from_classes(grad_query_block, dilation_step, frame_count, row_count, col_count)
        )
        terms = jnp.stack([grad_key_block, grad_value_block], 0).reshape(
            2,
            dilation_step,
            dilation_step,
            key_frames,
            class_rows,
            class_cols,
            group_size,
            head_size,
        )
        partial_sum = jnp.transpose(terms, (0, 3, 4, 1, 5, 2, 6, 7)).reshape(tile_shape)
        returned_parts.append(retract(partial_sum, 2, row_reach, row_count, row_back))
    kv_grads = retract(
        jnp.concatenate(returned_parts, axis=4), 1, frame_reach, frame_count, frame_back
    )

    def restore(array):
        return jnp.take(array, head_restore, axis=3).reshape(
            frame_count, row_count, col_count, width
        )

    attended = restore(jnp.concatenate(attended_parts, axis=3))
    grad_queries = restore(jnp.concatenate(grad_query_parts, axis=3)).astype(jnp.bfloat16)
    grad_keys = restore(kv_grads[0]).astype(jnp.bfloat16)
    grad_values = restore(kv_grads[1]).astype(jnp.bfloat16)
    return (attended, grad_queries, grad_keys, grad_values)


def solution(mesh):
    placed = (
        P("tm", "space", None, None),
        P("tm", "space", None, None),
        P("tm", "space", None, None),
        P("tm", "space", None, None),
        P(),
    )
    return jax.shard_map(
        shards,
        mesh=mesh,
        in_specs=placed,
        out_specs=(
            P("tm", "space", None, None),
            P("tm", "space", None, None),
            P("tm", "space", None, None),
            P("tm", "space", None, None),
        ),
        check_vma=False,
    )
```

profile of v0, /device:TPU:9, one launch (start us, length us, event | category | flops | bytes accessed | tf_op | source)
XLA Modules:
  0.0 738.7 jit_solution(8553045640913200934)
XLA Ops:
  14.3 4.8 collective-permute-start.2
  19.1 4.0 collective-permute-start.1
  23.1 4.6 collective-permute-start
  43.7 6.2 and.258
  49.9 3.0 collective-permute-done
  58.4 5.2 collective-permute-done.3
  68.1 8.8 %collective-permute-start.6 = (bf16[2,7,3,8,2,64]{5,3,2,4,1,0:T(8,128)(2,1)S(1)}, bf16[2,7,3,8,2,64]{5,3,2,4,1,0:T(8,128)(2,1)S(1)}, u32[]{:S(2)}, u32[]{:S(2)}) collective-permute-start(bf16[2,7,3,8,2,64]{5,3,2,4,1,0:T(8,128)(2,1)S(1)} %get-tuple-element.20), channel_id=1, source_target_pairs={{0,1},{1,2},{2,3},{3,4},{4,5},{5,6},{6,7},{7,8},{8,9},{9,10},{10,1... | collective-permute-start | bytes 258056 | tf_op jit(solution)/shard_map/ppermute | solution.py:13
  76.9 5.4 collective-permute-start.7
  84.7 5.3 collective-permute-start.8
  90.0 4.8 collective-permute-start.9
  94.8 4.4 collective-permute-start.10
  99.2 5.9 collective-permute-start.11
  120.5 5.5 collective-permute-start.12
  126.0 3.7 collective-permute-start.13
  129.7 3.9 collective-permute-done.9
  142.6 2.4 multiply_reduce_fusion.1
  146.8 3.0 copy.124
  149.8 27.7 %collective-permute-done.10 = bf16[2,7,12,8,4,64]{5,3,2,4,1,0:T(8,128)(2,1)} collective-permute-done((bf16[2,7,12,8,4,64]{5,3,2,4,1,0:T(8,128)(2,1)}, bf16[2,7,12,8,4,64]{5,3,2,4,1,0:T(8,128)(2,1)}, u32[]{:S(2)}, u32[]{:S(2)}) %collective-permute-start.10) | collective-permute-done | bytes 688160 | tf_op jit(solution)/shard_map/ppermute | solution.py:13
  177.5 35.9 %collective-permute-done.11 = bf16[2,7,12,8,4,64]{5,3,2,4,1,0:T(8,128)(2,1)} collective-permute-done((bf16[2,7,12,8,4,64]{5,3,2,4,1,0:T(8,128)(2,1)}, bf16[2,7,12,8,4,64]{5,3,2,4,1,0:T(8,128)(2,1)}, u32[]{:S(2)}, u32[]{:S(2)}) %collective-permute-start.11) | collective-permute-done | bytes 688160 | tf_op jit(solution)/shard_map/ppermute | solution.py:13
  213.3 2.3 pad_maximum_fusion.1
  216.6 3.6 fusion.65
  220.2 2.3 copy.94
  222.4 5.1 copy.95
  230.4 2.3 copy.90
  232.7 6.5 copy.96
  239.1 4.5 convolution_bitcast_fusion.1
  243.6 3.8 multiply_reduce_fusion
  247.4 7.8 %copy.128 = f32[4,4,140,4,64]{4,3,2,1,0:T(4,128)} copy(f32[4,4,140,4,64]{2,4,3,1,0:T(8,128)} %convolution_bitcast_fusion.1) | data formatting | bytes 4587520 | tf_op jit(solution)/shard_map/abhqk,abqhe->abkhe/transpose | solution.py:257
  257.3 2.8 multiply_bitcast_fusion
  260.1 8.2 %copy.127 = f32[4,4,140,4,64]{4,3,2,1,0:T(4,128)} copy(f32[4,4,140,4,64]{2,4,3,1,0:T(8,128)} %multiply_bitcast_fusion) | data formatting | bytes 4587520 | tf_op jit(solution)/shard_map/mul | solution.py:254
  268.3 9.7 %maximum_bitcast_fusion = f32[2,7,10,4,2,4,4,64]{7,6,4,2,1,5,3,0:T(4,128)} fusion(f32[1,4,4,7,10,2,4,64]{7,6,5,4,3,2,1,0:T(4,128)} %bitcast.274, f32[1,4,4,7,10,2,4,64]{7,6,5,4,3,2,1,0:T(4,128)} %bitcast.275), kind=kLoop, calls=%fused_computation.11 | loop fusion | flops 1146880 | bytes 9175040 | tf_op jit(solution)/shard_map/transpose | solution.py:273
  278.1 10.8 %copy.129 = f32[2,7,10,4,2,4,4,64]{7,5,4,6,3,2,1,0:T(4,128)} copy(f32[2,7,10,4,2,4,4,64]{7,6,4,2,1,5,3,0:T(4,128)} %maximum_bitcast_fusion) | data formatting | bytes 9175040 | tf_op jit(solution)/shard_map/transpose | solution.py:273
  288.8 3.4 fusion.63
  292.3 64.7 %collective-permute-start.16 = (f32[2,7,12,8,4,64]{5,3,4,2,1,0:T(8,128)S(1)}, f32[2,7,12,8,4,64]{5,3,4,2,1,0:T(8,128)S(1)}, u32[]{:S(2)}, u32[]{:S(2)}) collective-permute-start(f32[2,7,12,8,4,64]{5,3,4,2,1,0:T(8,128)S(1)} %get-tuple-element.11), channel_id=1, source_target_pairs={{1,0},{2,1},{3,2},{4,3},{5,4},{6,5},{7,6},{8,7},{9,8},{10,9},{11,1... | collective-permute-start | bytes 4128776 | tf_op jit(solution)/shard_map/ppermute | solution.py:13
  359.9 2.2 collective-permute-start.15
  362.1 8.2 %collective-permute-start.14 = (f32[2,7,6,8,2,64]{5,3,4,2,1,0:T(8,128)S(1)}, f32[2,7,6,8,2,64]{5,3,4,2,1,0:T(8,128)S(1)}, u32[]{:S(2)}, u32[]{:S(2)}) collective-permute-start(f32[2,7,6,8,2,64]{5,3,4,2,1,0:T(8,128)S(1)} %get-tuple-element.29), channel_id=1, source_target_pairs={{1,0},{2,1},{3,2},{4,3},{5,4},{6,5},{7,6},{8,7},{9,8},{10,9},{11,1... | collective-permute-start | bytes 1032200 | tf_op jit(solution)/shard_map/ppermute | solution.py:13
  370.3 2.1 collective-permute-start.17
  374.5 242.6 %collective-permute-done.14 = f32[2,7,6,8,2,64]{5,3,4,2,1,0:T(8,128)S(1)} collective-permute-done((f32[2,7,6,8,2,64]{5,3,4,2,1,0:T(8,128)S(1)}, f32[2,7,6,8,2,64]{5,3,4,2,1,0:T(8,128)S(1)}, u32[]{:S(2)}, u32[]{:S(2)}) %collective-permute-start.14) | collective-permute-done | bytes 344096 | tf_op jit(solution)/shard_map/ppermute | solution.py:13
  618.6 2.9 collective-permute-done.17
  623.4 2.7 fusion.64
  628.2 2.3 collective-permute-start.18
  633.2 24.2 %collective-permute-start.23 = (f32[2,1,16,8,8,64]{5,3,4,2,1,0:T(8,128)}, f32[2,1,16,8,8,64]{5,3,4,2,1,0:T(8,128)S(1)}, u32[]{:S(2)}, u32[]{:S(2)}) collective-permute-start(f32[2,1,16,8,8,64]{5,3,4,2,1,0:T(8,128)} %get-tuple-element.13), channel_id=1, source_target_pairs={{0,48},{16,64},{32,80},{48,96},{64,112},{80,128},{96,144},{112,160... | collective-permute-start | bytes 1572872 | tf_op jit(solution)/shard_map/ppermute | solution.py:13
  658.7 6.5 collective-permute-start.21
  666.5 19.7 %collective-permute-done.18 = f32[2,1,16,8,8,64]{5,3,4,2,1,0:T(8,128)} collective-permute-done((f32[2,1,16,8,8,64]{5,3,4,2,1,0:T(8,128)}, f32[2,1,16,8,8,64]{5,3,4,2,1,0:T(8,128)}, u32[]{:S(2)}, u32[]{:S(2)}) %collective-permute-start.18) | collective-permute-done | bytes 524320 | tf_op jit(solution)/shard_map/ppermute | solution.py:13
  691.2 10.8 %collective-permute-done.22 = f32[2,1,16,8,8,64]{5,3,4,2,1,0:T(8,128)} collective-permute-done((f32[2,1,16,8,8,64]{5,3,4,2,1,0:T(8,128)}, f32[2,1,16,8,8,64]{5,3,4,2,1,0:T(8,128)}, u32[]{:S(2)}, u32[]{:S(2)}) %collective-permute-start.22) | collective-permute-done | bytes 524320 | tf_op jit(solution)/shard_map/ppermute | solution.py:13
  702.0 11.3 %collective-permute-done.21 = f32[2,1,16,8,8,64]{5,3,4,2,1,0:T(8,128)} collective-permute-done((f32[2,1,16,8,8,64]{5,3,4,2,1,0:T(8,128)}, f32[2,1,16,8,8,64]{5,3,4,2,1,0:T(8,128)}, u32[]{:S(2)}, u32[]{:S(2)}) %collective-permute-start.21) | collective-permute-done | bytes 524320 | tf_op jit(solution)/shard_map/ppermute | solution.py:13
  713.3 15.7 %collective-permute-done.20 = f32[2,1,16,8,8,64]{5,3,4,2,1,0:T(8,128)} collective-permute-done((f32[2,1,16,8,8,64]{5,3,4,2,1,0:T(8,128)}, f32[2,1,16,8,8,64]{5,3,4,2,1,0:T(8,128)}, u32[]{:S(2)}, u32[]{:S(2)}) %collective-permute-start.20) | collective-permute-done | bytes 524320 | tf_op jit(solution)/shard_map/ppermute | solution.py:13
  729.0 3.6 fusion.29
  (234 shorter events, 99.5 us)
Async XLA Ops:
  0.6 7.4 %copy-start.20 = (bf16[1,16,8,512]{3,2,1,0:T(8,128)(2,1)S(1)}, bf16[1,16,8,512]{3,2,1,0:T(8,128)(2,1)}, u32[]{:S(2)}) copy-start(bf16[1,16,8,512]{3,2,1,0:T(8,128)(2,1)} %param.11) | copy-start | bytes 393220
  3.8 5.2 copy-start.21
  10.7 20.5 %copy-start.12 = (bf16[1,16,8,8,64]{4,2,1,3,0:T(8,128)(2,1)}, bf16[1,16,8,8,64]{4,2,1,3,0:T(8,128)(2,1)S(1)}, u32[]{:S(2)}) copy-start(bf16[1,16,8,8,64]{4,2,1,3,0:T(8,128)(2,1)S(1)} %get-tuple-element.45) | copy-start | bytes 393220
  11.7 53.2 %collective-permute-start.5 = (bf16[2,1,16,8,8,64]{5,3,2,4,1,0:T(8,128)(2,1)}, bf16[2,1,16,8,8,64]{5,3,2,4,1,0:T(8,128)(2,1)}, u32[]{:S(2)}, u32[]{:S(2)}) collective-permute-start(bf16[2,1,16,8,8,64]{5,3,2,4,1,0:T(8,128)(2,1)} %pad_maximum_fusion.4), channel_id=1, source_target_pairs={{48,0},{64,16},{80,32},{96,48},{112,64},{128,80},{144,96},{160,112... | collective-permute-start | bytes 786440 | tf_op jit(solution)/shard_map/ppermute | solution.py:13
  13.0 50.8 %collective-permute-start.4 = (bf16[2,1,16,8,8,64]{5,3,2,4,1,0:T(8,128)(2,1)}, bf16[2,1,16,8,8,64]{5,3,2,4,1,0:T(8,128)(2,1)}, u32[]{:S(2)}, u32[]{:S(2)}) collective-permute-start(bf16[2,1,16,8,8,64]{5,3,2,4,1,0:T(8,128)(2,1)} %pad_maximum_fusion.4), channel_id=1, source_target_pairs={{32,0},{48,16},{64,32},{80,48},{96,64},{112,80},{128,96},{144,112}... | collective-permute-start | bytes 786440 | tf_op jit(solution)/shard_map/ppermute | solution.py:13
  14.3 42.8 %collective-permute-start.2 = (bf16[2,1,16,8,8,64]{5,3,2,4,1,0:T(8,128)(2,1)}, bf16[2,1,16,8,8,64]{5,3,2,4,1,0:T(8,128)(2,1)}, u32[]{:S(2)}, u32[]{:S(2)}) collective-permute-start(bf16[2,1,16,8,8,64]{5,3,2,4,1,0:T(8,128)(2,1)} %pad_maximum_fusion.4), channel_id=1, source_target_pairs={{0,16},{16,32},{32,48},{48,64},{64,80},{80,96},{96,112},{112,128},... | collective-permute-start | bytes 786440 | tf_op jit(solution)/shard_map/ppermute | solution.py:13
  19.1 36.9 %collective-permute-start.1 = (bf16[2,1,16,8,8,64]{5,3,2,4,1,0:T(8,128)(2,1)}, bf16[2,1,16,8,8,64]{5,3,2,4,1,0:T(8,128)(2,1)}, u32[]{:S(2)}, u32[]{:S(2)}) collective-permute-start(bf16[2,1,16,8,8,64]{5,3,2,4,1,0:T(8,128)(2,1)} %pad_maximum_fusion.4), channel_id=1, source_target_pairs={{0,32},{16,48},{32,64},{48,80},{64,96},{80,112},{96,128},{112,144}... | collective-permute-start | bytes 786440 | tf_op jit(solution)/shard_map/ppermute | solution.py:13
  23.1 29.8 %collective-permute-start = (bf16[2,1,16,8,8,64]{5,3,2,4,1,0:T(8,128)(2,1)}, bf16[2,1,16,8,8,64]{5,3,2,4,1,0:T(8,128)(2,1)}, u32[]{:S(2)}, u32[]{:S(2)}) collective-permute-start(bf16[2,1,16,8,8,64]{5,3,2,4,1,0:T(8,128)(2,1)} %pad_maximum_fusion.4), channel_id=1, source_target_pairs={{0,48},{16,64},{32,80},{48,96},{64,112},{80,128},{96,144},{112,160... | collective-permute-start | bytes 786440 | tf_op jit(solution)/shard_map/ppermute | solution.py:13
  53.0 10.7 %collective-permute-start.3 = (bf16[2,1,16,8,8,64]{5,3,2,4,1,0:T(8,128)(2,1)}, bf16[2,1,16,8,8,64]{5,3,2,4,1,0:T(8,128)(2,1)S(1)}, u32[]{:S(2)}, u32[]{:S(2)}) collective-permute-start(bf16[2,1,16,8,8,64]{5,3,2,4,1,0:T(8,128)(2,1)} %pad_maximum_fusion.4), channel_id=1, source_target_pairs={{16,0},{32,16},{48,32},{64,48},{80,64},{96,80},{112,96},{128,112},... | collective-permute-start | bytes 786440 | tf_op jit(solution)/shard_map/ppermute | solution.py:13
  68.1 31.1 %collective-permute-start.6 = (bf16[2,7,3,8,2,64]{5,3,2,4,1,0:T(8,128)(2,1)S(1)}, bf16[2,7,3,8,2,64]{5,3,2,4,1,0:T(8,128)(2,1)S(1)}, u32[]{:S(2)}, u32[]{:S(2)}) collective-permute-start(bf16[2,7,3,8,2,64]{5,3,2,4,1,0:T(8,128)(2,1)S(1)} %get-tuple-element.20), channel_id=1, source_target_pairs={{0,1},{1,2},{2,3},{3,4},{4,5},{5,6},{6,7},{7,8},{8,9},{9,10},{10,1... | collective-permute-start | bytes 258056 | tf_op jit(solution)/shard_map/ppermute | solution.py:13
  76.9 28.2 %collective-permute-start.7 = (bf16[2,7,3,8,2,64]{5,3,2,4,1,0:T(8,128)(2,1)S(1)}, bf16[2,7,3,8,2,64]{5,3,2,4,1,0:T(8,128)(2,1)S(1)}, u32[]{:S(2)}, u32[]{:S(2)}) collective-permute-start(bf16[2,7,3,8,2,64]{5,3,2,4,1,0:T(8,128)(2,1)S(1)} %get-tuple-element.21), channel_id=1, source_target_pairs={{1,0},{2,1},{3,2},{4,3},{5,4},{6,5},{7,6},{8,7},{9,8},{10,9},{11,1... | collective-permute-start | bytes 258056 | tf_op jit(solution)/shard_map/ppermute | solution.py:13
  84.7 41.3 %collective-permute-start.8 = (bf16[2,7,6,8,2,64]{5,3,2,4,1,0:T(8,128)(2,1)}, bf16[2,7,6,8,2,64]{5,3,2,4,1,0:T(8,128)(2,1)}, u32[]{:S(2)}, u32[]{:S(2)}) collective-permute-start(bf16[2,7,6,8,2,64]{5,3,2,4,1,0:T(8,128)(2,1)} %get-tuple-element.24), channel_id=1, source_target_pairs={{0,1},{1,2},{2,3},{3,4},{4,5},{5,6},{6,7},{7,8},{8,9},{9,10},{10,1... | collective-permute-start | bytes 516104 | tf_op jit(solution)/shard_map/ppermute | solution.py:13
  90.0 43.7 %collective-permute-start.9 = (bf16[2,7,6,8,2,64]{5,3,2,4,1,0:T(8,128)(2,1)}, bf16[2,7,6,8,2,64]{5,3,2,4,1,0:T(8,128)(2,1)}, u32[]{:S(2)}, u32[]{:S(2)}) collective-permute-start(bf16[2,7,6,8,2,64]{5,3,2,4,1,0:T(8,128)(2,1)} %get-tuple-element.25), channel_id=1, source_target_pairs={{1,0},{2,1},{3,2},{4,3},{5,4},{6,5},{7,6},{8,7},{9,8},{10,9},{11,1... | collective-permute-start | bytes 516104 | tf_op jit(solution)/shard_map/ppermute | solution.py:13
  94.8 82.7 %collective-permute-start.10 = (bf16[2,7,12,8,4,64]{5,3,2,4,1,0:T(8,128)(2,1)}, bf16[2,7,12,8,4,64]{5,3,2,4,1,0:T(8,128)(2,1)}, u32[]{:S(2)}, u32[]{:S(2)}) collective-permute-start(bf16[2,7,12,8,4,64]{5,3,2,4,1,0:T(8,128)(2,1)} %get-tuple-element.26), channel_id=1, source_target_pairs={{0,1},{1,2},{2,3},{3,4},{4,5},{5,6},{6,7},{7,8},{8,9},{9,10},{10,1... | collective-permute-start | bytes 2064392 | tf_op jit(solution)/shard_map/ppermute | solution.py:13
  99.2 114.1 %collective-permute-start.11 = (bf16[2,7,12,8,4,64]{5,3,2,4,1,0:T(8,128)(2,1)}, bf16[2,7,12,8,4,64]{5,3,2,4,1,0:T(8,128)(2,1)}, u32[]{:S(2)}, u32[]{:S(2)}) collective-permute-start(bf16[2,7,12,8,4,64]{5,3,2,4,1,0:T(8,128)(2,1)} %get-tuple-element.27), channel_id=1, source_target_pairs={{1,0},{2,1},{3,2},{4,3},{5,4},{6,5},{7,6},{8,7},{9,8},{10,9},{11,1... | collective-permute-start | bytes 2064392 | tf_op jit(solution)/shard_map/ppermute | solution.py:13
  105.5 4.5 copy-start.6
  120.5 249.7 %collective-permute-start.12 = (f32[2,7,3,8,2,64]{5,3,4,2,1,0:T(8,128)}, f32[2,7,3,8,2,64]{5,3,4,2,1,0:T(8,128)}, u32[]{:S(2)}, u32[]{:S(2)}) collective-permute-start(f32[2,7,3,8,2,64]{5,3,4,2,1,0:T(8,128)} %copy.147), channel_id=1, source_target_pairs={{1,0},{2,1},{3,2},{4,3},{5,4},{6,5},{7,6},{8,7},{9,8},{10,9},{11,1... | collective-permute-start | bytes 516104 | tf_op jit(solution)/shard_map/ppermute | solution.py:13
  126.0 247.4 %collective-permute-start.13 = (f32[2,7,3,8,2,64]{5,3,4,2,1,0:T(8,128)}, f32[2,7,3,8,2,64]{5,3,4,2,1,0:T(8,128)}, u32[]{:S(2)}, u32[]{:S(2)}) collective-permute-start(f32[2,7,3,8,2,64]{5,3,4,2,1,0:T(8,128)} %copy.148), channel_id=1, source_target_pairs={{0,1},{1,2},{2,3},{3,4},{4,5},{5,6},{6,7},{7,8},{8,9},{9,10},{10,1... | collective-permute-start | bytes 516104 | tf_op jit(solution)/shard_map/ppermute | solution.py:13
  145.4 70.3 %copy-start.14 = (bf16[2,2,2,32,392]{4,3,2,1,0:T(8,128)(2,1)}, bf16[2,2,2,32,392]{4,3,2,1,0:T(8,128)(2,1)S(1)}, u32[]{:S(2)}) copy-start(bf16[2,2,2,32,392]{4,3,2,1,0:T(8,128)(2,1)S(1)} %fusion.21) | copy-start | bytes 602116
  145.4 68.0 %copy-start.3 = (bf16[2,7,16,8,4,64]{5,3,2,4,1,0:T(8,128)(2,1)S(1)}, bf16[2,7,16,8,4,64]{5,3,2,4,1,0:T(8,128)(2,1)}, u32[]{:S(2)}) copy-start(bf16[2,7,16,8,4,64]{5,3,2,4,1,0:T(8,128)(2,1)} %slice.224) | copy-start | bytes 2752516
  222.4 5.1 copy-start.11
  247.4 7.8 %copy-start.17 = (bf16[4,4,1,4,2,4,64]{6,4,3,5,1,0,2:T(2,128)(2,1)S(1)}, bf16[4,4,1,4,2,4,64]{6,4,3,5,1,0,2:T(2,128)(2,1)}, u32[]{:S(2)}) copy-start(bf16[4,4,1,4,2,4,64]{6,4,3,5,1,0,2:T(2,128)(2,1)} %copy.112) | copy-start | bytes 196612
  247.4 7.8 %copy-start.19 = (f32[4,4,4,8]{3,2,1,0:T(4,128)S(1)}, f32[4,4,4,8]{3,2,1,0:T(4,128)}, u32[]{:S(2)}) copy-start(f32[4,4,4,8]{3,2,1,0:T(4,128)} %get-tuple-element.53) | copy-start | bytes 6148
  247.4 7.8 %copy-start.29 = (f32[4,4,8,4]{2,3,1,0:T(4,128)S(1)}, f32[4,4,8,4]{2,3,1,0:T(4,128)}, u32[]{:S(2)}) copy-start(f32[4,4,8,4]{2,3,1,0:T(4,128)} %get-tuple-element.55) | copy-start | bytes 6148
  288.8 68.1 %copy-start.4 = (f32[2,2,392,2,64]{4,2,3,1,0:T(8,128)S(1)}, f32[2,2,392,2,64]{4,2,3,1,0:T(8,128)}, u32[]{:S(2)}) copy-start(f32[2,2,392,2,64]{4,2,3,1,0:T(8,128)} %copy.125) | copy-start | bytes 2408452
  288.8 68.1 %copy-start.5 = (f32[2,2,392,2,64]{4,2,3,1,0:T(8,128)S(1)}, f32[2,2,392,2,64]{4,2,3,1,0:T(8,128)}, u32[]{:S(2)}) copy-start(f32[2,2,392,2,64]{4,2,3,1,0:T(8,128)} %copy.124) | copy-start | bytes 2408452
  292.3 325.6 %collective-permute-start.16 = (f32[2,7,12,8,4,64]{5,3,4,2,1,0:T(8,128)S(1)}, f32[2,7,12,8,4,64]{5,3,4,2,1,0:T(8,128)S(1)}, u32[]{:S(2)}, u32[]{:S(2)}) collective-permute-start(f32[2,7,12,8,4,64]{5,3,4,2,1,0:T(8,128)S(1)} %get-tuple-element.11), channel_id=1, source_target_pairs={{1,0},{2,1},{3,2},{4,3},{5,4},{6,5},{7,6},{8,7},{9,8},{10,9},{11,1... | collective-permute-start | bytes 4128776 | tf_op jit(solution)/shard_map/ppermute | solution.py:13
  357.8 259.6 %slice-start = ((s8[9175040]{0:T(1024)(128)(4,1)}), s8[4194304]{0:T(1024)(128)(4,1)S(1)}, s32[]{:S(2)}) async-start(s8[9175040]{0:T(1024)(128)(4,1)} %bitcast.270), calls=%async_computation | async-start | bytes 8388608
  357.8 259.6 %slice-start.1 = ((s8[9175040]{0:T(1024)(128)(4,1)}), s8[786432]{0:T(1024)(128)(4,1)S(1)}, s32[]{:S(2)}) async-start(s8[9175040]{0:T(1024)(128)(4,1)} %bitcast.270), calls=%async_computation.1 | async-start | bytes 1572864
  359.6 12.8 %copy-start.2 = (f32[2,7,16,8,2,64]{5,3,4,2,1,0:T(8,128)S(1)}, f32[2,7,16,8,2,64]{5,3,4,2,1,0:T(8,128)}, u32[]{:S(2)}) copy-start(f32[2,7,16,8,2,64]{5,3,4,2,1,0:T(8,128)} %copy.145) | copy-start | bytes 2752516
  359.6 12.8 %copy-start.10 = (f32[2,7,3,8,2,64]{5,3,2,1,4,0:T(8,128)S(1)}, f32[2,7,3,8,2,64]{5,3,2,1,4,0:T(8,128)}, u32[]{:S(2)}) copy-start(f32[2,7,3,8,2,64]{5,3,2,1,4,0:T(8,128)} %get-tuple-element.31) | copy-start | bytes 516100
  359.8 257.6 %slice-start.2 = ((s8[9175040]{0:T(1024)(128)(4,1)}), s8[4194304]{0:T(1024)(128)(4,1)S(1)}, s32[]{:S(2)}) async-start(s8[9175040]{0:T(1024)(128)(4,1)} %bitcast.270), calls=%async_computation.2 | async-start | bytes 8388608
  359.9 257.3 %collective-permute-start.15 = (f32[2,7,6,8,2,64]{5,3,4,2,1,0:T(8,128)S(1)}, f32[2,7,6,8,2,64]{5,3,4,2,1,0:T(8,128)S(1)}, u32[]{:S(2)}, u32[]{:S(2)}) collective-permute-start(f32[2,7,6,8,2,64]{5,3,4,2,1,0:T(8,128)S(1)} %get-tuple-element.28), channel_id=1, source_target_pairs={{0,1},{1,2},{2,3},{3,4},{4,5},{5,6},{6,7},{7,8},{8,9},{9,10},{10,1... | collective-permute-start | bytes 1032200 | tf_op jit(solution)/shard_map/ppermute | solution.py:13
  362.1 255.0 %collective-permute-start.14 = (f32[2,7,6,8,2,64]{5,3,4,2,1,0:T(8,128)S(1)}, f32[2,7,6,8,2,64]{5,3,4,2,1,0:T(8,128)S(1)}, u32[]{:S(2)}, u32[]{:S(2)}) collective-permute-start(f32[2,7,6,8,2,64]{5,3,4,2,1,0:T(8,128)S(1)} %get-tuple-element.29), channel_id=1, source_target_pairs={{1,0},{2,1},{3,2},{4,3},{5,4},{6,5},{7,6},{8,7},{9,8},{10,9},{11,1... | collective-permute-start | bytes 1032200 | tf_op jit(solution)/shard_map/ppermute | solution.py:13
  370.3 251.2 %collective-permute-start.17 = (f32[2,7,12,8,4,64]{5,3,4,2,1,0:T(8,128)S(1)}, f32[2,7,12,8,4,64]{5,3,4,2,1,0:T(8,128)S(1)}, u32[]{:S(2)}, u32[]{:S(2)}) collective-permute-start(f32[2,7,12,8,4,64]{5,3,4,2,1,0:T(8,128)S(1)} %get-tuple-element.10), channel_id=1, source_target_pairs={{0,1},{1,2},{2,3},{3,4},{4,5},{5,6},{6,7},{7,8},{8,9},{9,10},{10,1... | collective-permute-start | bytes 4128776 | tf_op jit(solution)/shard_map/ppermute | solution.py:13
  623.3 4.8 copy-start
  623.4 7.2 copy-start.7
  623.4 7.2 copy-start.9
  623.4 7.7 %copy-start.26 = (bf16[1,1,128,2,64]{2,4,3,1,0:T(8,128)(2,1)S(1)}, bf16[1,1,128,2,64]{2,4,3,1,0:T(8,128)(2,1)}, u32[]{:S(2)}) copy-start(bf16[1,1,128,2,64]{2,4,3,1,0:T(8,128)(2,1)} %get-tuple-element.64) | copy-start | bytes 98308
  628.2 4.4 copy-start.25
  628.2 58.0 %collective-permute-start.18 = (f32[2,1,16,8,8,64]{5,3,4,2,1,0:T(8,128)}, f32[2,1,16,8,8,64]{5,3,4,2,1,0:T(8,128)}, u32[]{:S(2)}, u32[]{:S(2)}) collective-permute-start(f32[2,1,16,8,8,64]{5,3,4,2,1,0:T(8,128)} %get-tuple-element.12), channel_id=1, source_target_pairs={{16,0},{32,16},{48,32},{64,48},{80,64},{96,80},{112,96},{128,112},... | collective-permute-start | bytes 1572872 | tf_op jit(solution)/shard_map/ppermute | solution.py:13
  631.2 57.7 %copy-start.22 = (bf16[4,4,4,64,8]{3,4,2,1,0:T(8,128)(2,1)S(1)}, bf16[4,4,4,64,8]{3,4,2,1,0:T(8,128)(2,1)}, u32[]{:S(2)}) copy-start(bf16[4,4,4,64,8]{3,4,2,1,0:T(8,128)(2,1)} %get-tuple-element.56) | copy-start | bytes 196612
  632.4 56.5 %copy-start.27 = (s32[1024]{0:T(1024)S(1)}, s32[1024]{0:T(1024)}, u32[]{:S(2)}) copy-start(s32[1024]{0:T(1024)} %get-tuple-element.67) | copy-start | bytes 12292
  633.2 58.0 %collective-permute-start.23 = (f32[2,1,16,8,8,64]{5,3,4,2,1,0:T(8,128)}, f32[2,1,16,8,8,64]{5,3,4,2,1,0:T(8,128)S(1)}, u32[]{:S(2)}, u32[]{:S(2)}) collective-permute-start(f32[2,1,16,8,8,64]{5,3,4,2,1,0:T(8,128)} %get-tuple-element.13), channel_id=1, source_target_pairs={{0,48},{16,64},{32,80},{48,96},{64,112},{80,128},{96,144},{112,160... | collective-permute-start | bytes 1572872 | tf_op jit(solution)/shard_map/ppermute | solution.py:13
  657.4 44.6 %collective-permute-start.22 = (f32[2,1,16,8,8,64]{5,3,4,2,1,0:T(8,128)}, f32[2,1,16,8,8,64]{5,3,4,2,1,0:T(8,128)}, u32[]{:S(2)}, u32[]{:S(2)}) collective-permute-start(f32[2,1,16,8,8,64]{5,3,4,2,1,0:T(8,128)} %get-tuple-element.14), channel_id=1, source_target_pairs={{48,0},{64,16},{80,32},{96,48},{112,64},{128,80},{144,96},{160,112... | collective-permute-start | bytes 1572872 | tf_op jit(solution)/shard_map/ppermute | solution.py:13
  658.7 54.6 %collective-permute-start.21 = (f32[2,1,16,8,8,64]{5,3,4,2,1,0:T(8,128)}, f32[2,1,16,8,8,64]{5,3,4,2,1,0:T(8,128)}, u32[]{:S(2)}, u32[]{:S(2)}) collective-permute-start(f32[2,1,16,8,8,64]{5,3,4,2,1,0:T(8,128)} %get-tuple-element.15), channel_id=1, source_target_pairs={{0,32},{16,48},{32,64},{48,80},{64,96},{80,112},{96,128},{112,144}... | collective-permute-start | bytes 1572872 | tf_op jit(solution)/shard_map/ppermute | solution.py:13
  665.2 63.8 %collective-permute-start.20 = (f32[2,1,16,8,8,64]{5,3,4,2,1,0:T(8,128)}, f32[2,1,16,8,8,64]{5,3,4,2,1,0:T(8,128)}, u32[]{:S(2)}, u32[]{:S(2)}) collective-permute-start(f32[2,1,16,8,8,64]{5,3,4,2,1,0:T(8,128)} %get-tuple-element.16), channel_id=1, source_target_pairs={{32,0},{48,16},{64,32},{80,48},{96,64},{112,80},{128,96},{144,112}... | collective-permute-start | bytes 1572872 | tf_op jit(solution)/shard_map/ppermute | solution.py:13
  686.2 42.8 %collective-permute-start.19 = (f32[2,1,16,8,8,64]{5,3,4,2,1,0:T(8,128)}, f32[2,1,16,8,8,64]{5,3,4,2,1,0:T(8,128)}, u32[]{:S(2)}, u32[]{:S(2)}) collective-permute-start(f32[2,1,16,8,8,64]{5,3,4,2,1,0:T(8,128)} %get-tuple-element.17), channel_id=1, source_target_pairs={{0,16},{16,32},{32,48},{48,64},{64,80},{80,96},{96,112},{112,128},... | collective-permute-start | bytes 1572872 | tf_op jit(solution)/shard_map/ppermute | solution.py:13
  (9 other events, 17.1 us)
where the time goes:
time: 749 us; the launch traced here: 739 us
  waiting for transfers between devices  379 us (51%)
  starting transfers between devices  176 us (23%)
  local copies, waits for them, and re-layouts  114 us (15%)
  other arithmetic  37.9 us (5%)
  matrix products  29.4 us (4%)
    ppermute x24, waiting for transfers between devices, passed_along(): lax.ppermute(value, axis, [(source, source + steps) for source in range(i...  379 us
    ppermute x24, starting transfers between devices, passed_along(): lax.ppermute(value, axis, [(source, source + steps) for source in range(i...  176 us
  transfers between devices with their start and end apart: 24, of which 11 were waited for; matrix products, arithmetic and copies ran while one was open for 20% of the time, Pallas kernels for 0%

commit v1 on v0

v1 whole, which is shorter than its diff:
```python
import functools

import jax
import jax.numpy as jnp
from jax import lax
from jax.experimental import pallas as pl
from jax.experimental.pallas import tpu as pltpu
from jax.sharding import PartitionSpec as P

HEADS = 8
WIDTH = 64
ROWS = 16
COLS = 8
RING = 8
REACH = 3
SPAN = 16
CELL = ROWS * COLS
HALO = 12
EDGE = HALO * COLS
MESH = pl.DeviceIdType.MESH
F32 = jnp.float32
BF16 = jnp.bfloat16

HALO_ROWS = (12, 12, 12, 12, 4, 4, 6, 6)
GROUP_ROWS = (12, 4, 6)


def slot_device(slot):
    return 2 * lax.rem(slot, 4) + lax.div(slot, 4)


def head_ranks(dilation):
    steps = [dilation[h] for h in range(HEADS)]
    ranks = []
    for h in range(HEADS):
        rank = jnp.int32(0)
        for other in range(HEADS):
            before = steps[other] <= steps[h] if other < h else steps[other] < steps[h]
            if other != h:
                rank = rank + jnp.where(before, 1, 0)
        ranks.append(rank)
    return ranks


def low_lanes(rows):
    return lax.broadcasted_iota(jnp.int32, (rows, 2 * WIDTH), 1) < WIDTH


def pack_kernel(dilation, query, key, value, grad, packed):
    ranks = head_ranks(dilation)
    low = low_lanes(CELL)
    for slot in range(HEADS):
        head = jnp.int32(0)
        for h in range(HEADS):
            head = head + jnp.where(ranks[h] == (slot + 4) % HEADS, h, 0)
        odd = lax.rem(head, 2) == 1
        lanes = pl.ds(pl.multiple_of(lax.div(head, 2) * 2 * WIDTH, 2 * WIDTH), 2 * WIDTH)
        for place, (first, second) in enumerate(((key, value), (query, grad))):
            a = first[:, lanes].astype(F32)
            b = second[:, lanes].astype(F32)
            a = jnp.where(odd, pltpu.roll(a, WIDTH, 1), a)
            b = jnp.where(odd, b, pltpu.roll(b, WIDTH, 1))
            packed[slot, place] = jnp.where(low, a, b).astype(BF16)


def unpack_kernel(dilation, result, attended, grad_query, grad_key, grad_value):
    ranks = head_ranks(dilation)
    low = low_lanes(CELL)
    for block in range(HEADS // 2):
        slots = [lax.rem(ranks[2 * block + i] + 4, HEADS) for i in range(2)]
        lanes = pl.ds(block * 2 * WIDTH, 2 * WIDTH)
        for place, (first, second) in enumerate(((grad_key, grad_value), (grad_query, attended))):
            a = result[slots[0], place].astype(F32)
            b = result[slots[1], place].astype(F32)
            first[:, lanes] = jnp.where(low, a, pltpu.roll(b, WIDTH, 1)).astype(BF16)
            second[:, lanes] = jnp.where(low, pltpu.roll(a, WIDTH, 1), b).astype(BF16)


def for_each(count, body):
    def step(i, carry):
        body(i)
        return carry

    lax.fori_loop(0, count, step, 0)


def main_kernel(
    rings,
    blocks,
    packed,
    result,
    halo,
    main,
    hstage,
    keys,
    quers,
    bias,
    scores,
    probs,
    total,
    gmain,
    ghalo,
    rmain,
    rmain_b,
    rhalo,
    rhalo_b,
    hsum,
    rrow,
    final,
    row_send,
    row_recv,
    main_send,
    main_next,
    main_recv,
    halo_send,
    halo_next,
    halo_recv,
    gmain_send,
    gmain_recv,
    gmain_recv_b,
    ghalo_send,
    ghalo_recv,
    ghalo_recv_b,
    back_send,
    back_recv,
):
    tm = lax.axis_index("tm")
    space = lax.axis_index("space")
    ring = lax.div(tm, RING)
    me = lax.rem(tm, RING)
    my_slot = lax.rem(me, 2) * 4 + lax.div(me, 2)
    group = jnp.where(lax.rem(me, 2) == 0, 0, jnp.where(me < 4, 1, 2))
    step = jnp.where(group == 0, 4, group)
    has_down = ring > 0
    has_up = ring < rings - 1
    has_prev = space > 0
    has_next = space < blocks - 1
    to_down = has_down & (me <= 2)
    to_up = has_up & (me >= 5)
    shared = to_down | to_up

    def by_group(body):
        for number, rows in enumerate(GROUP_ROWS):
            pl.when(group == number)(functools.partial(body, rows))

    def send(source, target, send_sem, recv_sem, where):
        return pltpu.make_async_remote_copy(
            src_ref=source,
            dst_ref=target,
            send_sem=send_sem,
            recv_sem=recv_sem,
            device_id=where,
            device_id_type=MESH,
        )

    def arrived(ref, sem):
        pltpu.make_async_copy(ref, ref, sem).wait()

    barrier = pltpu.get_barrier_semaphore()

    def greet(i):
        def hello(where):
            pl.semaphore_signal(barrier, inc=1, device_id=where, device_id_type=MESH)

        pl.when(i != me)(lambda: hello({"tm": ring * RING + i}))
        pl.when(has_down & ((me <= 2) | (i >= 5)))(lambda: hello({"tm": (ring - 1) * RING + i}))
        pl.when(has_up & ((me >= 5) | (i <= 2)))(lambda: hello({"tm": (ring + 1) * RING + i}))

    for_each(RING, greet)

    @pl.when(has_prev)
    def _():
        pl.semaphore_signal(barrier, inc=1, device_id={"space": space - 1}, device_id_type=MESH)

    @pl.when(has_next)
    def _():
        pl.semaphore_signal(barrier, inc=1, device_id={"space": space + 1}, device_id_type=MESH)

    greeted = (
        RING
        - 1
        + jnp.where(has_down, jnp.where(me <= 2, RING, 3), 0)
        + jnp.where(has_up, jnp.where(me >= 5, RING, 3), 0)
        + jnp.where(has_prev, 1, 0)
        + jnp.where(has_next, 1, 0)
    )
    pl.semaphore_wait(barrier, greeted)

    def row_copies(slot):
        size = HALO_ROWS[slot] * COLS
        upward = send(
            packed.at[slot, 0, pl.ds(CELL - size, size)],
            halo.at[slot, pl.ds(EDGE - size, size)],
            row_send.at[slot, 0],
            row_recv.at[slot, 0],
            {"space": space + 1},
        )
        downward = send(
            packed.at[slot, 0, pl.ds(0, size)],
            halo.at[slot, pl.ds(EDGE, size)],
            row_send.at[slot, 1],
            row_recv.at[slot, 1],
            {"space": space - 1},
        )
        return upward, downward

    for slot in range(HEADS):
        upward, downward = row_copies(slot)
        pl.when(has_next)(upward.start)
        pl.when(has_prev)(downward.start)

    def main_copies(slot):
        where = slot_device(slot)
        at_home = send(
            packed.at[slot], main.at[me + 4], main_send.at[slot], main_recv.at[me + 3],
            {"tm": ring * RING + where},
        )
        local = pltpu.make_async_copy(packed.at[slot], main.at[me + 4], main_recv.at[me + 3])
        down = send(
            packed.at[slot, 0], main.at[me + 12, 0], main_next.at[slot], main_recv.at[me + 11],
            {"tm": (ring - 1) * RING + where},
        )
        up = send(
            packed.at[slot, 0], main.at[me - 4, 0], main_next.at[slot], main_recv.at[me - 5],
            {"tm": (ring + 1) * RING + where},
        )
        return where, at_home, local, down, up

    def main_start(slot):
        where, at_home, local, down, up = main_copies(slot)
        pl.when(where != me)(lambda: at_home.start())
        pl.when(where == me)(lambda: local.start())
        pl.when(to_down)(lambda: down.start())
        pl.when(to_up)(lambda: up.start())

    for_each(HEADS, main_start)

    def clear(first, count):
        def one(i):
            main[first + i, 0] = jnp.zeros((CELL, 2 * WIDTH), BF16)
            hstage[first + i] = jnp.zeros((2 * EDGE, 2 * WIDTH), BF16)

        for_each(count, one)

    clear(0, 1)
    clear(15, 1)
    pl.when(jnp.logical_not(has_down))(lambda: clear(1, 3))
    pl.when(jnp.logical_not(has_up))(lambda: clear(12, 3))

    def clear_halo(first):
        def one(slot):
            halo[slot, pl.ds(first, EDGE)] = jnp.zeros((EDGE, 2 * WIDTH), BF16)

        for_each(HEADS, one)

    pl.when(jnp.logical_not(has_prev))(lambda: clear_halo(0))
    pl.when(jnp.logical_not(has_next))(lambda: clear_halo(EDGE))

    def clear_total(i):
        total[i] = jnp.zeros((2 * WIDTH, 2 * WIDTH), F32)

    for_each(2 * HALO + ROWS, clear_total)

    shape = (RING * COLS, SPAN * COLS)
    query_at = lax.broadcasted_iota(jnp.int32, shape, 0)
    key_at = lax.broadcasted_iota(jnp.int32, shape, 1)
    frame_apart = lax.shift_right_logical(key_at, 3) - lax.shift_right_logical(query_at, 3) - 4
    key_frame = lax.shift_right_logical(key_at, 3) + ring * RING - 4
    col_apart = (key_at & 7) - (query_at & 7)
    seen = (
        (jnp.abs(frame_apart) <= REACH)
        & (key_frame >= 0)
        & (key_frame < rings * RING)
        & (jnp.abs(col_apart) <= REACH * step)
        & ((col_apart & (step - 1)) == 0)
    )
    bias[0] = jnp.where(seen, 0.0, -1e30)
    bias[1] = jnp.full(shape, -1e30, F32)

    def halo_copies(slot):
        size = HALO_ROWS[slot] * COLS
        where = 2 * (slot % 4) + slot // 4
        part = pl.ds(EDGE - size, 2 * size)
        source = halo.at[slot, part]
        at_home = send(
            source, hstage.at[me + 4, part], halo_send.at[slot], halo_recv.at[me + 3],
            {"tm": ring * RING + where},
        )
        local = pltpu.make_async_copy(source, hstage.at[me + 4, part], halo_recv.at[me + 3])
        down = send(
            source, hstage.at[me + 12, part], halo_next.at[slot], halo_recv.at[me + 11],
            {"tm": (ring - 1) * RING + where},
        )
        up = send(
            source, hstage.at[me - 4, part], halo_next.at[slot], halo_recv.at[me - 5],
            {"tm": (ring + 1) * RING + where},
        )
        return where, at_home, local, down, up

    for slot in range(HEADS):
        upward, downward = row_copies(slot)
        pl.when(has_prev)(upward.wait_recv)
        pl.when(has_next)(downward.wait_recv)
        where, at_home, local, down, up = halo_copies(slot)
        pl.when(me != where)(at_home.start)
        pl.when(me == where)(local.start)
        pl.when(to_down)(down.start)
        pl.when(to_up)(up.start)

    def main_wait(i):
        arrived(main.at[i + 4], main_recv.at[i + 3])

    for_each(RING, main_wait)

    def main_wait_down(i):
        arrived(main.at[i + 1, 0], main_recv.at[i])

    pl.when(has_down)(lambda: for_each(3, main_wait_down))

    def main_wait_up(i):
        arrived(main.at[i + 12, 0], main_recv.at[i + 11])

    pl.when(has_up)(lambda: for_each(3, main_wait_up))

    def two_rows(part, frames):
        wide = part.astype(F32).reshape(frames, 2, COLS, 2 * WIDTH)
        return [
            wide[:, i].reshape(frames * COLS, 2 * WIDTH).astype(BF16) for i in range(2)
        ]

    def turn_main(pair):
        rows = pl.ds(pl.multiple_of(pair * 16, 16), 16)
        even, odd = two_rows(main[:, 0, rows], SPAN)
        keys[HALO + 2 * pair] = even
        keys[HALO + 2 * pair + 1] = odd
        even, odd = two_rows(main[pl.ds(4, RING), 1, rows], RING)
        quers[2 * pair] = even
        quers[2 * pair + 1] = odd

    for_each(ROWS // 2, turn_main)

    def halo_wait(rows):
        part = pl.ds(EDGE - rows * COLS, 2 * rows * COLS)

        def one(i):
            arrived(hstage.at[i + 1, part], halo_recv.at[i])

        def some(first, count):
            for_each(count, lambda i: one(first + i))

        some(3, RING)
        pl.when(has_down)(lambda: some(0, 3))
        pl.when(has_up)(lambda: some(11, 3))

    by_group(halo_wait)

    def turn_halo(pair):
        rows = pl.ds(pl.multiple_of(pair * 16, 16), 16)
        even, odd = two_rows(hstage[:, rows], SPAN)
        place = 2 * pair + jnp.where(pair < HALO // 2, 0, ROWS)
        keys[place] = even
        keys[place + 1] = odd

    for_each(HALO, turn_halo)

    low = low_lanes(RING * COLS)
    wide = SPAN * COLS
    tall = RING * COLS
    scale = WIDTH ** -0.5 * 1.4426950408889634
    for half in range(2):
        probs[pl.ds(0, tall), pl.ds(7 * wide, wide)] = jnp.zeros((tall, wide), BF16)
        probs[pl.ds(tall, tall), pl.ds(0, wide)] = jnp.zeros((tall, wide), BF16)
        probs[pl.ds(2 * tall, tall), pl.ds(7 * wide, wide)] = jnp.zeros((tall, wide), BF16)
        probs[pl.ds(3 * tall, tall), pl.ds(0, wide)] = jnp.zeros((tall, wide), BF16)

    def attend(i):
        first = lax.div(i, step) * (2 * step) + lax.rem(i, step)
        pair = [quers[first], quers[first + step]]
        none = jnp.zeros_like(pair[0])
        left = jnp.concatenate(
            [jnp.where(low, q, none) for q in pair] + [jnp.where(low, none, q) for q in pair], 0
        )
        places = [first + HALO + step * (j - REACH) for j in range(8)]
        block = jnp.concatenate([keys[place] for place in places], 0)
        scores[...] = lax.dot_general(
            left, block, (((1,), (1,)), ((), ())), preferred_element_type=F32
        )
        outside = []
        for place in places:
            row = place - HALO + space * ROWS
            outside.append(jnp.where((row < 0) | (row >= blocks * ROWS), 1, 0))
        chunk = 16
        for half in range(2):
            for start in range(0, tall, chunk):
                rows = pl.ds(half * tall + start, chunk)
                grad_rows = pl.ds((2 + half) * tall + start, chunk)
                tiles = range(half, half + 7)
                raw = [
                    scores[rows, pl.ds(j * wide, wide)]
                    + bias[outside[j], pl.ds(start, chunk)]
                    for j in tiles
                ]
                peak = jnp.max(functools.reduce(jnp.maximum, raw), axis=1, keepdims=True)
                power = [jnp.exp2((tile - peak) * scale) for tile in raw]
                gains = [scores[grad_rows, pl.ds(j * wide, wide)] for j in tiles]
                summed = jnp.sum(functools.reduce(jnp.add, power), axis=1, keepdims=True)
                inverse = 1.0 / summed
                delta = inverse * jnp.sum(
                    functools.reduce(jnp.add, [a * b for a, b in zip(power, gains)]),
                    axis=1,
                    keepdims=True,
                )
                for j, a, b in zip(tiles, power, gains):
                    weight = a * inverse
                    probs[grad_rows, pl.ds(j * wide, wide)] = weight.astype(BF16)
                    probs[rows, pl.ds(j * wide, wide)] = (weight * (b - delta)).astype(BF16)
        both = probs[...]
        out = jnp.dot(both, block, preferred_element_type=F32)
        for half in range(2):
            grad_query = out[half * tall : (half + 1) * tall] * WIDTH ** -0.5
            attended = out[(2 + half) * tall : (3 + half) * tall]
            quers[first + half * step] = jnp.where(low, grad_query, attended).astype(BF16)
        back = lax.dot_general(left, both, (((0,), (0,)), ((), ())), preferred_element_type=F32)
        for j, place in enumerate(places):
            total[place] += back[:, j * wide : (j + 1) * wide]

    for_each(ROWS // 2, attend)

    low_all = low_lanes(SPAN * COLS)

    def key_row(place):
        turned = total[place].T
        return jnp.where(low_all, turned * WIDTH ** -0.5, turned).reshape(SPAN, COLS, 2 * WIDTH)

    def back_halo(pair):
        place = 2 * pair + jnp.where(pair < HALO // 2, 0, ROWS)
        both = jnp.concatenate([key_row(place), key_row(place + 1)], 1)
        ghalo[:, pl.ds(pl.multiple_of(pair * 16, 16), 16)] = both.astype(BF16)

    for_each(HALO, back_halo)

    def ghalo_copies(rows, i):
        part = pl.ds(EDGE - rows * COLS, 2 * rows * COLS)
        source = ghalo.at[i + 1, part]
        at_home = send(
            source, rhalo.at[my_slot, part], ghalo_send.at[i], ghalo_recv.at[my_slot],
            {"tm": ring * RING + i - 3},
        )
        local = pltpu.make_async_copy(source, rhalo.at[my_slot, part], ghalo_recv.at[my_slot])
        down = send(
            source, rhalo_b.at[my_slot, part], ghalo_send.at[i], ghalo_recv_b.at[my_slot],
            {"tm": (ring - 1) * RING + i + 5},
        )
        up = send(
            source, rhalo_b.at[my_slot, part], ghalo_send.at[i], ghalo_recv_b.at[my_slot],
            {"tm": (ring + 1) * RING + i - 11},
        )
        return at_home, local, down, up

    def ghalo_start(rows):
        def at_home(i):
            pl.when(i != me)(lambda: ghalo_copies(rows, i + 3)[0].start())
            pl.when(i == me)(lambda: ghalo_copies(rows, i + 3)[1].start())

        for_each(RING, at_home)
        pl.when(has_down)(lambda: for_each(3, lambda i: ghalo_copies(rows, i)[2].start()))
        pl.when(has_up)(lambda: for_each(3, lambda i: ghalo_copies(rows, i + 11)[3].start()))

    by_group(ghalo_start)

    def back_main(pair):
        rows = pl.ds(pl.multiple_of(pair * 16, 16), 16)
        place = HALO + 2 * pair
        both = jnp.concatenate([key_row(place), key_row(place + 1)], 1)
        gmain[:, 0, rows] = both.astype(BF16)
        outs = [
            quers[2 * pair + i].astype(F32).reshape(RING, COLS, 2 * WIDTH) for i in range(2)
        ]
        gmain[pl.ds(4, RING), 1, rows] = jnp.concatenate(outs, 1).astype(BF16)

    for_each(ROWS // 2, back_main)

    def gmain_copies(i):
        at_home = send(
            gmain.at[i + 1], rmain.at[my_slot], gmain_send.at[i], gmain_recv.at[my_slot],
            {"tm": ring * RING + i - 3},
        )
        local = pltpu.make_async_copy(gmain.at[i + 1], rmain.at[my_slot], gmain_recv.at[my_slot])
        down = send(
            gmain.at[i + 1, 0], rmain_b.at[my_slot], gmain_send.at[i], gmain_recv_b.at[my_slot],
            {"tm": (ring - 1) * RING + i + 5},
        )
        up = send(
            gmain.at[i + 1, 0], rmain_b.at[my_slot], gmain_send.at[i], gmain_recv_b.at[my_slot],
            {"tm": (ring + 1) * RING + i - 11},
        )
        return at_home, local, down, up

    def gmain_start(i):
        pl.when(i != me)(lambda: gmain_copies(i + 3)[0].start())
        pl.when(i == me)(lambda: gmain_copies(i + 3)[1].start())

    for_each(RING, gmain_start)
    pl.when(has_down)(lambda: for_each(3, lambda i: gmain_copies(i)[2].start()))
    pl.when(has_up)(lambda: for_each(3, lambda i: gmain_copies(i + 11)[3].start()))

    def back_copies(slot):
        size = HALO_ROWS[slot] * COLS
        lower = pl.ds(EDGE - size, size)
        upper = pl.ds(EDGE, size)
        downward = send(
            hsum.at[slot, lower], rrow.at[slot, lower], back_send.at[slot, 0],
            back_recv.at[slot, 0], {"space": space - 1},
        )
        upward = send(
            hsum.at[slot, upper], rrow.at[slot, upper], back_send.at[slot, 1],
            back_recv.at[slot, 1], {"space": space + 1},
        )
        return downward, upward

    for slot in range(HEADS):
        size = HALO_ROWS[slot] * COLS
        part = pl.ds(EDGE - size, 2 * size)
        arrived(rhalo.at[slot, part], ghalo_recv.at[slot])

        @pl.when(shared)
        def _():
            arrived(rhalo_b.at[slot, part], ghalo_recv_b.at[slot])
            both = rhalo[slot, part].astype(F32) + rhalo_b[slot, part].astype(F32)
            hsum[slot, part] = both.astype(BF16)

        @pl.when(jnp.logical_not(shared))
        def _():
            hsum[slot, part] = rhalo[slot, part]

        downward, upward = back_copies(slot)
        pl.when(has_prev)(downward.start)
        pl.when(has_next)(upward.start)

    for slot in range(HEADS):
        size = HALO_ROWS[slot] * COLS
        arrived(rmain.at[slot], gmain_recv.at[slot])
        final[...] = rmain[slot, 0].astype(F32)

        @pl.when(shared)
        def _():
            arrived(rmain_b.at[slot], gmain_recv_b.at[slot])
            final[...] += rmain_b[slot].astype(F32)

        downward, upward = back_copies(slot)

        @pl.when(has_next)
        def _():
            downward.wait_recv()
            final[pl.ds(CELL - size, size)] += rrow[slot, pl.ds(EDGE - size, size)].astype(F32)

        @pl.when(has_prev)
        def _():
            upward.wait_recv()
            final[pl.ds(0, size)] += rrow[slot, pl.ds(EDGE, size)].astype(F32)

        result[slot, 0] = final[...].astype(BF16)
        result[slot, 1] = rmain[slot, 1]

    for slot in range(HEADS):
        upward, downward = row_copies(slot)
        pl.when(has_next)(upward.wait_send)
        pl.when(has_prev)(downward.wait_send)
        where, at_home, local, down, up = halo_copies(slot)
        pl.when(me != where)(at_home.wait_send)
        pl.when(to_down)(down.wait_send)
        pl.when(to_up)(up.wait_send)
        downward, upward = back_copies(slot)
        pl.when(has_prev)(downward.wait_send)
        pl.when(has_next)(upward.wait_send)

    def main_sent(slot):
        where, at_home, local, down, up = main_copies(slot)
        pl.when(where != me)(lambda: at_home.wait_send())
        pl.when(to_down)(lambda: down.wait_send())
        pl.when(to_up)(lambda: up.wait_send())

    for_each(HEADS, main_sent)

    def gmain_sent(i):
        pl.when(i != me)(lambda: gmain_copies(i + 3)[0].wait_send())

    for_each(RING, gmain_sent)
    pl.when(has_down)(lambda: for_each(3, lambda i: gmain_copies(i)[2].wait_send()))
    pl.when(has_up)(lambda: for_each(3, lambda i: gmain_copies(i + 11)[3].wait_send()))

    def ghalo_sent(rows):
        def at_home(i):
            pl.when(i != me)(lambda: ghalo_copies(rows, i + 3)[0].wait_send())

        for_each(RING, at_home)
        pl.when(has_down)(lambda: for_each(3, lambda i: ghalo_copies(rows, i)[2].wait_send()))
        pl.when(has_up)(lambda: for_each(3, lambda i: ghalo_copies(rows, i + 11)[3].wait_send()))

    by_group(ghalo_sent)


def shards(queries, key_vectors, values, cotangent, dilation):
    frames, rows, cols, width = queries.shape
    flat = [a.reshape(CELL, width) for a in (queries, key_vectors, values, cotangent)]
    smem = pl.BlockSpec(memory_space=pltpu.SMEM)
    vmem = pl.BlockSpec(memory_space=pltpu.VMEM)
    lanes = 2 * WIDTH
    packed = pl.pallas_call(
        pack_kernel,
        out_shape=jax.ShapeDtypeStruct((HEADS, 2, CELL, lanes), BF16),
        in_specs=[smem, vmem, vmem, vmem, vmem],
        out_specs=vmem,
        name="pack_heads",
    )(dilation, *flat)
    dma = pltpu.SemaphoreType.DMA
    result = pl.pallas_call(
        functools.partial(main_kernel, lax.axis_size("tm") // RING, lax.axis_size("space")),
        out_shape=jax.ShapeDtypeStruct((HEADS, 2, CELL, lanes), BF16),
        in_specs=[vmem],
        out_specs=vmem,
        scratch_shapes=[
            pltpu.VMEM((HEADS, 2 * EDGE, lanes), BF16),
            pltpu.VMEM((SPAN, 2, CELL, lanes), BF16),
            pltpu.VMEM((SPAN, 2 * EDGE, lanes), BF16),
            pltpu.VMEM((ROWS + 2 * HALO, SPAN * COLS, lanes), BF16),
            pltpu.VMEM((ROWS, RING * COLS, lanes), BF16),
            pltpu.VMEM((2, RING * COLS, SPAN * COLS), F32),
            pltpu.VMEM((4 * RING * COLS, 8 * SPAN * COLS), F32),
            pltpu.VMEM((4 * RING * COLS, 8 * SPAN * COLS), BF16),
            pltpu.VMEM((ROWS + 2 * HALO, lanes, SPAN * COLS), F32),
            pltpu.VMEM((SPAN, 2, CELL, lanes), BF16),
            pltpu.VMEM((SPAN, 2 * EDGE, lanes), BF16),
            pltpu.VMEM((HEADS, 2, CELL, lanes), BF16),
            pltpu.VMEM((HEADS, CELL, lanes), BF16),
            pltpu.VMEM((HEADS, 2 * EDGE, lanes), BF16),
            pltpu.VMEM((HEADS, 2 * EDGE, lanes), BF16),
            pltpu.VMEM((HEADS, 2 * EDGE, lanes), BF16),
            pltpu.VMEM((HEADS, 2 * EDGE, lanes), BF16),
            pltpu.VMEM((CELL, lanes), F32),
            dma((HEADS, 2)),
            dma((HEADS, 2)),
            dma((HEADS,)),
            dma((HEADS,)),
            dma((14,)),
            dma((HEADS,)),
            dma((HEADS,)),
            dma((14,)),
            dma((14,)),
            dma((HEADS,)),
            dma((HEADS,)),
            dma((14,)),
            dma((HEADS,)),
            dma((HEADS,)),
            dma((HEADS, 2)),
            dma((HEADS, 2)),
        ],
        compiler_params=pltpu.CompilerParams(
            collective_id=0, has_side_effects=True, vmem_limit_bytes=40 * 1024 * 1024
        ),
        name="neighbourhood_attention",
    )(packed)
    outs = pl.pallas_call(
        unpack_kernel,
        out_shape=[jax.ShapeDtypeStruct((CELL, width), BF16)] * 4,
        in_specs=[smem, vmem],
        out_specs=[vmem] * 4,
        name="unpack_heads",
    )(dilation, result)
    return tuple(a.reshape(frames, rows, cols, width) for a in outs)


def solution(mesh):
    placed = P("tm", "space", None, None)
    return jax.shard_map(
        shards,
        mesh=mesh,
        in_specs=(placed, placed, placed, placed, P()),
        out_specs=(placed, placed, placed, placed),
        check_vma=False,
    )
```

time: 749 us -> 75.3 us (0.10)
  the two profiles are of different devices: /device:TPU:9 before, /device:TPU:89 now
where the time goes in v1:
time: 75.3 us; the launch traced here: 75.1 us
  Pallas kernels  72.7 us (97%)
  local copies, waits for them, and re-layouts  1.83 us (2%)
    pallas_call x1, Pallas kernels, shards(): pl.pallas_call(functools.partial(main_kernel, lax.axis_size('tm') // RING...  68.2 us
    pallas_call x1, Pallas kernels, shards(): pl.pallas_call(pack_kernel, out_shape=jax.ShapeDtypeStruct((HEADS, 2, CEL...  2.37 us
    pallas_call x1, Pallas kernels, shards(): pl.pallas_call(unpack_kernel, out_shape=[jax.ShapeDtypeStruct((CELL, widt...  2.07 us
    unnamed x4, local copies, waits for them, and re-layouts  1.83 us

profile of v1, /device:TPU:89, one launch (start us, length us, event | category | flops | bytes accessed | tf_op | source)
XLA Modules:
  0.0 75.1 jit_solution(12821460413201653616)
XLA Ops:
  0.6 2.4 %pack_heads.1.packed = bf16[8,2,128,128]{3,2,1,0:T(8,128)(2,1)} custom-call(s32[8]{0:T(128)} %dilation.3, bf16[128,512]{1,0:T(8,128)(2,1)} %bitcast.8, bf16[128,512]{1,0:T(8,128)(2,1)} %bitcast.9, bf16[128,512]{1,0:T(8,128)(2,1)} %bitcast.10, bf16[128,512]{1,0:T(8,128)(2,1)} %bitcast.11), custom_call_target="tpu_custom_call" | custom-call | tf_op jit(solution)/shard_map/pack_heads/pallas_call | solution.py:609
  3.0 0.0 copy-start.1
  3.0 1.0 %copy-done.1 = bf16[8,2,128,128]{3,2,1,0:T(8,128)(2,1)S(1)} copy-done((bf16[8,2,128,128]{3,2,1,0:T(8,128)(2,1)S(1)}, bf16[8,2,128,128]{3,2,1,0:T(8,128)(2,1)}, u32[]{:S(2)}) %copy-start.1) | copy-done | bytes 524312
  4.0 68.2 %neighbourhood_attention.1.result = bf16[8,2,128,128]{3,2,1,0:T(8,128)(2,1)S(1)} custom-call(bf16[8,2,128,128]{3,2,1,0:T(8,128)(2,1)S(1)} %copy-done.1), custom_call_target="tpu_custom_call" | custom-call | tf_op jit(solution)/shard_map/neighbourhood_attention/pallas_call | solution.py:617
  72.3 0.0 copy-start
  72.3 0.8 %copy-done = bf16[8,2,128,128]{3,2,1,0:T(8,128)(2,1)} copy-done((bf16[8,2,128,128]{3,2,1,0:T(8,128)(2,1)}, bf16[8,2,128,128]{3,2,1,0:T(8,128)(2,1)S(1)}, u32[]{:S(2)}) %copy-start) | copy-done | bytes 524312
  73.1 2.1 %unpack_heads.1 = (bf16[128,512]{1,0:T(8,128)(2,1)}, bf16[128,512]{1,0:T(8,128)(2,1)}, bf16[128,512]{1,0:T(8,128)(2,1)}, bf16[128,512]{1,0:T(8,128)(2,1)}) custom-call(s32[8]{0:T(128)} %dilation.3, bf16[8,2,128,128]{3,2,1,0:T(8,128)(2,1)} %copy-done), custom_call_target="tpu_custom_call" | custom-call | tf_op jit(solution)/shard_map/unpack_heads/pallas_call | solution.py:663
Async XLA Ops:
  3.0 1.0 %copy-start.1 = (bf16[8,2,128,128]{3,2,1,0:T(8,128)(2,1)S(1)}, bf16[8,2,128,128]{3,2,1,0:T(8,128)(2,1)}, u32[]{:S(2)}) copy-start(bf16[8,2,128,128]{3,2,1,0:T(8,128)(2,1)} %pack_heads.1.packed) | copy-start | bytes 1572868
  72.3 0.8 %copy-start = (bf16[8,2,128,128]{3,2,1,0:T(8,128)(2,1)}, bf16[8,2,128,128]{3,2,1,0:T(8,128)(2,1)S(1)}, u32[]{:S(2)}) copy-start(bf16[8,2,128,128]{3,2,1,0:T(8,128)(2,1)S(1)} %neighbourhood_attention.1.result) | copy-start | bytes 1572868

commit v2 on v1

v2 whole, which is shorter than its diff:
```python
import functools

import jax
import jax.numpy as jnp
from jax import lax
from jax.experimental import pallas as pl
from jax.experimental.pallas import tpu as pltpu
from jax.sharding import PartitionSpec as P

HEADS = 8
WIDTH = 64
ROWS = 16
COLS = 8
RING = 8
REACH = 3
SPAN = 16
CELL = ROWS * COLS
HALO = 12
EDGE = HALO * COLS
MESH = pl.DeviceIdType.MESH
F32 = jnp.float32
BF16 = jnp.bfloat16

HALO_ROWS = (12, 12, 12, 12, 4, 4, 6, 6)
GROUP_ROWS = (12, 4, 6)


def slot_device(slot):
    return 2 * lax.rem(slot, 4) + lax.div(slot, 4)


def head_ranks(dilation):
    steps = [dilation[h] for h in range(HEADS)]
    ranks = []
    for h in range(HEADS):
        rank = jnp.int32(0)
        for other in range(HEADS):
            before = steps[other] <= steps[h] if other < h else steps[other] < steps[h]
            if other != h:
                rank = rank + jnp.where(before, 1, 0)
        ranks.append(rank)
    return ranks


def low_lanes(rows):
    return lax.broadcasted_iota(jnp.int32, (rows, 2 * WIDTH), 1) < WIDTH


def pick(ref, chosen):
    width = 2 * WIDTH
    block = ref[:, pl.ds(0, width)]
    for number in range(1, HEADS // 2):
        here = chosen[2 * number] | chosen[2 * number + 1]
        block = jnp.where(here, ref[:, pl.ds(number * width, width)], block)
    return block.astype(F32)


def pack(dilation, first, second, packed, place):
    ranks = head_ranks(dilation)
    low = low_lanes(CELL)
    for slot in range(HEADS):
        chosen = [ranks[h] == (slot + 4) % HEADS for h in range(HEADS)]
        odd = chosen[1] | chosen[3] | chosen[5] | chosen[7]
        a = pick(first, chosen)
        b = pick(second, chosen)
        a = jnp.where(odd, pltpu.roll(a, WIDTH, 1), a)
        b = jnp.where(odd, b, pltpu.roll(b, WIDTH, 1))
        packed[slot, place] = jnp.where(low, a, b).astype(BF16)


def unpack_kernel(
    dilation_in,
    result_in,
    attended_out,
    grad_query_out,
    grad_key_out,
    grad_value_out,
    dilation,
    result,
    attended,
    grad_query,
    grad_key,
    grad_value,
    load,
    store,
):
    loads = [
        pltpu.make_async_copy(result_in.at[slot], result.at[slot], load.at[slot])
        for slot in range(HEADS)
    ]
    loads.append(pltpu.make_async_copy(dilation_in, dilation, load.at[HEADS]))
    for copy in loads:
        copy.start()
    for copy in loads:
        copy.wait()
    ranks = head_ranks(dilation)
    low = low_lanes(CELL)
    pairs = ((grad_key, grad_value), (grad_query, attended))
    outs = ((grad_key_out, grad_value_out), (grad_query_out, attended_out))
    stores = []
    for place in range(2):
        first, second = pairs[place]
        for block in range(HEADS // 2):
            slots = [lax.rem(ranks[2 * block + i] + 4, HEADS) for i in range(2)]
            lanes = pl.ds(block * 2 * WIDTH, 2 * WIDTH)
            a = result[slots[0], place].astype(F32)
            b = result[slots[1], place].astype(F32)
            first[:, lanes] = jnp.where(low, a, pltpu.roll(b, WIDTH, 1)).astype(BF16)
            second[:, lanes] = jnp.where(low, pltpu.roll(a, WIDTH, 1), b).astype(BF16)
        for i in range(2):
            copy = pltpu.make_async_copy(pairs[place][i], outs[place][i], store.at[2 * place + i])
            copy.start()
            stores.append(copy)
    for copy in stores:
        copy.wait()


def for_each(count, body):
    def step(i, carry):
        body(i)
        return carry

    lax.fori_loop(0, count, step, 0)


def main_kernel(
    rings,
    blocks,
    dilation_in,
    query_in,
    key_in,
    value_in,
    grad_in,
    output,
    dilation,
    query,
    key,
    value,
    grad,
    packed,
    main,
    hstage,
    keys,
    quers,
    bias,
    scores,
    probs,
    total,
    gmain,
    ghalo,
    cmain,
    chalo,
    rmain,
    rhalo,
    final,
    result,
    load,
    store,
    main_send,
    main_recv,
    halo_send,
    halo_recv,
    near_send,
    near_recv,
    gmain_send,
    gmain_recv,
    ghalo_send,
    ghalo_recv,
    gnear_send,
    gnear_recv,
):
    tm = lax.axis_index("tm")
    space = lax.axis_index("space")
    ring = lax.div(tm, RING)
    me = lax.rem(tm, RING)
    my_slot = lax.rem(me, 2) * 4 + lax.div(me, 2)
    group = jnp.where(lax.rem(me, 2) == 0, 0, jnp.where(me < 4, 1, 2))
    step = jnp.where(group == 0, 4, group)
    has_down = ring > 0
    has_up = ring < rings - 1
    has_prev = space > 0
    has_next = space < blocks - 1

    def by_group(body):
        for number, rows in enumerate(GROUP_ROWS):
            pl.when(group == number)(functools.partial(body, rows))

    def send(source, target, send_sem, recv_sem, where):
        return pltpu.make_async_remote_copy(
            src_ref=source,
            dst_ref=target,
            send_sem=send_sem,
            recv_sem=recv_sem,
            device_id=where,
            device_id_type=MESH,
        )

    def arrived(ref, sem):
        pltpu.make_async_copy(ref, ref, sem).wait()

    loads = [
        pltpu.make_async_copy(source, target, load.at[number])
        for number, (source, target) in enumerate(
            (
                (dilation_in, dilation),
                (key_in, key),
                (value_in, value),
                (query_in, query),
                (grad_in, grad),
            )
        )
    ]
    for copy in loads:
        copy.start()

    barrier = pltpu.get_barrier_semaphore()

    def hello(where):
        pl.semaphore_signal(barrier, inc=1, device_id=where, device_id_type=MESH)

    def greet(i):
        there = ring * RING + i
        pl.when(i != me)(lambda: hello({"tm": there}))
        pl.when(has_prev)(lambda: hello({"tm": there, "space": space - 1}))
        pl.when(has_next)(lambda: hello({"tm": there, "space": space + 1}))

    for_each(RING, greet)
    pl.when(has_down)(lambda: hello({"tm": tm - RING}))
    pl.when(has_up)(lambda: hello({"tm": tm + RING}))
    for copy in loads[:3]:
        copy.wait()
    pack(dilation, key, value, packed, 0)
    greeted = (
        RING
        - 1
        + jnp.where(has_down, 1, 0)
        + jnp.where(has_up, 1, 0)
        + jnp.where(has_prev, RING, 0)
        + jnp.where(has_next, RING, 0)
    )
    pl.semaphore_wait(barrier, greeted)

    def halo_copies(slot):
        size = HALO_ROWS[slot] * COLS
        there = ring * RING + 2 * (slot % 4) + slot // 4
        upward = send(
            packed.at[slot, 0, pl.ds(CELL - size, size)],
            hstage.at[me + 4, pl.ds(EDGE - size, size)],
            halo_send.at[slot, 0],
            halo_recv.at[me, 0],
            {"tm": there, "space": space + 1},
        )
        downward = send(
            packed.at[slot, 0, pl.ds(0, size)],
            hstage.at[me + 4, pl.ds(EDGE, size)],
            halo_send.at[slot, 1],
            halo_recv.at[me, 1],
            {"tm": there, "space": space - 1},
        )
        return upward, downward

    for slot in range(HEADS):
        upward, downward = halo_copies(slot)
        pl.when(has_next)(upward.start)
        pl.when(has_prev)(downward.start)

    for copy in loads[3:]:
        copy.wait()
    pack(dilation, query, grad, packed, 1)

    def main_copies(slot):
        where = slot_device(slot)
        at_home = send(
            packed.at[slot], main.at[me + 4], main_send.at[slot], main_recv.at[me],
            {"tm": ring * RING + where},
        )
        local = pltpu.make_async_copy(packed.at[slot], main.at[me + 4], main_recv.at[me])
        return where, at_home, local

    def main_start(slot):
        where, at_home, local = main_copies(slot)
        pl.when(where != me)(lambda: at_home.start())
        pl.when(where == me)(lambda: local.start())

    for_each(HEADS, main_start)

    def clear(first, count):
        def one(i):
            main[first + i, 0] = jnp.zeros((CELL, 2 * WIDTH), BF16)
            hstage[first + i] = jnp.zeros((2 * EDGE, 2 * WIDTH), BF16)

        for_each(count, one)

    clear(0, 1)
    clear(15, 1)
    pl.when(jnp.logical_not(has_down))(lambda: clear(1, 3))
    pl.when(jnp.logical_not(has_up))(lambda: clear(12, 3))

    def clear_halo(first):
        def one(i):
            hstage[i + 4, pl.ds(first, EDGE)] = jnp.zeros((EDGE, 2 * WIDTH), BF16)

        for_each(RING, one)

    pl.when(jnp.logical_not(has_prev))(lambda: clear_halo(0))
    pl.when(jnp.logical_not(has_next))(lambda: clear_halo(EDGE))

    def clear_total(i):
        total[i] = jnp.zeros((2 * WIDTH, 2 * WIDTH), F32)

    for_each(2 * HALO + ROWS, clear_total)

    shape = (RING * COLS, SPAN * COLS)
    query_at = lax.broadcasted_iota(jnp.int32, shape, 0)
    key_at = lax.broadcasted_iota(jnp.int32, shape, 1)
    frame_apart = lax.shift_right_logical(key_at, 3) - lax.shift_right_logical(query_at, 3) - 4
    key_frame = lax.shift_right_logical(key_at, 3) + ring * RING - 4
    col_apart = (key_at & 7) - (query_at & 7)
    seen = (
        (jnp.abs(frame_apart) <= REACH)
        & (key_frame >= 0)
        & (key_frame < rings * RING)
        & (jnp.abs(col_apart) <= REACH * step)
        & ((col_apart & (step - 1)) == 0)
    )
    bias[0] = jnp.where(seen, 0.0, -1e30)
    bias[1] = jnp.full(shape, -1e30, F32)

    def main_wait(i):
        arrived(main.at[i + 4], main_recv.at[i])

    def near_main():
        down = send(
            main.at[pl.ds(4, 3), 0], main.at[pl.ds(12, 3), 0], near_send.at[0], near_recv.at[0],
            {"tm": tm - RING},
        )
        up = send(
            main.at[pl.ds(9, 3), 0], main.at[pl.ds(1, 3), 0], near_send.at[1], near_recv.at[1],
            {"tm": tm + RING},
        )
        return down, up

    def near_halo(rows):
        part = pl.ds(EDGE - rows * COLS, 2 * rows * COLS)
        down = send(
            hstage.at[pl.ds(4, 3), part], hstage.at[pl.ds(12, 3), part],
            near_send.at[2], near_recv.at[2], {"tm": tm - RING},
        )
        up = send(
            hstage.at[pl.ds(9, 3), part], hstage.at[pl.ds(1, 3), part],
            near_send.at[3], near_recv.at[3], {"tm": tm + RING},
        )
        return down, up

    for_each(3, main_wait)
    pl.when(has_down)(lambda: near_main()[0].start())
    for_each(3, lambda i: main_wait(i + 5))
    pl.when(has_up)(lambda: near_main()[1].start())
    for_each(2, lambda i: main_wait(i + 3))

    def halo_phase(rows):
        size = rows * COLS

        def one(i):
            pl.when(has_prev)(
                lambda: arrived(hstage.at[i + 4, pl.ds(EDGE - size, size)], halo_recv.at[i, 0])
            )
            pl.when(has_next)(
                lambda: arrived(hstage.at[i + 4, pl.ds(EDGE, size)], halo_recv.at[i, 1])
            )

        for_each(3, one)
        pl.when(has_down)(lambda: near_halo(rows)[0].start())
        for_each(3, lambda i: one(i + 5))
        pl.when(has_up)(lambda: near_halo(rows)[1].start())
        for_each(2, lambda i: one(i + 3))

    by_group(halo_phase)
    pl.when(has_down)(lambda: near_main()[1].wait_recv())
    pl.when(has_up)(lambda: near_main()[0].wait_recv())

    def two_rows(part, frames):
        wide = part.astype(F32).reshape(frames, 2, COLS, 2 * WIDTH)
        return [wide[:, i].reshape(frames * COLS, 2 * WIDTH).astype(BF16) for i in range(2)]

    def turn_main(pair):
        rows = pl.ds(pl.multiple_of(pair * 16, 16), 16)
        even, odd = two_rows(main[:, 0, rows], SPAN)
        keys[HALO + 2 * pair] = even
        keys[HALO + 2 * pair + 1] = odd
        even, odd = two_rows(main[pl.ds(4, RING), 1, rows], RING)
        quers[2 * pair] = even
        quers[2 * pair + 1] = odd

    for_each(ROWS // 2, turn_main)

    def near_halo_wait(rows):
        pl.when(has_down)(lambda: near_halo(rows)[1].wait_recv())
        pl.when(has_up)(lambda: near_halo(rows)[0].wait_recv())

    by_group(near_halo_wait)

    def turn_halo(pair):
        rows = pl.ds(pl.multiple_of(pair * 16, 16), 16)
        even, odd = two_rows(hstage[:, rows], SPAN)
        place = 2 * pair + jnp.where(pair < HALO // 2, 0, ROWS)
        keys[place] = even
        keys[place + 1] = odd

    for_each(HALO, turn_halo)

    low = low_lanes(RING * COLS)
    wide = SPAN * COLS
    tall = RING * COLS
    scale = WIDTH ** -0.5 * 1.4426950408889634
    for part in range(4):
        unseen = pl.ds(0 if part % 2 else 7 * wide, wide)
        probs[pl.ds(part * tall, tall), unseen] = jnp.zeros((tall, wide), BF16)

    def attend(i):
        first = lax.div(i, step) * (2 * step) + lax.rem(i, step)
        pair = [quers[first], quers[first + step]]
        none = jnp.zeros_like(pair[0])
        left = jnp.concatenate(
            [jnp.where(low, q, none) for q in pair] + [jnp.where(low, none, q) for q in pair], 0
        )
        places = [first + HALO + step * (j - REACH) for j in range(8)]
        block = jnp.concatenate([keys[place] for place in places], 0)
        scores[...] = lax.dot_general(
            left, block, (((1,), (1,)), ((), ())), preferred_element_type=F32
        )
        outside = []
        for place in places:
            row = place - HALO + space * ROWS
            outside.append(jnp.where((row < 0) | (row >= blocks * ROWS), 1, 0))
        chunk = 16
        for half in range(2):
            for start in range(0, tall, chunk):
                rows = pl.ds(half * tall + start, chunk)
                grad_rows = pl.ds((2 + half) * tall + start, chunk)
                tiles = range(half, half + 7)
                raw = [
                    scores[rows, pl.ds(j * wide, wide)]
                    + bias[outside[j], pl.ds(start, chunk)]
                    for j in tiles
                ]
                peak = jnp.max(functools.reduce(jnp.maximum, raw), axis=1, keepdims=True)
                power = [jnp.exp2((tile - peak) * scale) for tile in raw]
                gains = [scores[grad_rows, pl.ds(j * wide, wide)] for j in tiles]
                summed = jnp.sum(functools.reduce(jnp.add, power), axis=1, keepdims=True)
                inverse = 1.0 / summed
                delta = inverse * jnp.sum(
                    functools.reduce(jnp.add, [a * b for a, b in zip(power, gains)]),
                    axis=1,
                    keepdims=True,
                )
                for j, a, b in zip(tiles, power, gains):
                    weight = a * inverse
                    probs[grad_rows, pl.ds(j * wide, wide)] = weight.astype(BF16)
                    probs[rows, pl.ds(j * wide, wide)] = (weight * (b - delta)).astype(BF16)
        both = probs[...]
        out = jnp.dot(both, block, preferred_element_type=F32)
        for half in range(2):
            grad_query = out[half * tall : (half + 1) * tall] * WIDTH ** -0.5
            attended = out[(2 + half) * tall : (3 + half) * tall]
            quers[first + half * step] = jnp.where(low, grad_query, attended).astype(BF16)
        back = lax.dot_general(left, both, (((0,), (0,)), ((), ())), preferred_element_type=F32)
        for j, place in enumerate(places):
            total[place] += back[:, j * wide : (j + 1) * wide]

    for_each(ROWS // 2, attend)

    low_all = low_lanes(SPAN * COLS)

    def key_row(place):
        turned = total[place].T
        return jnp.where(low_all, turned * WIDTH ** -0.5, turned).reshape(SPAN, COLS, 2 * WIDTH)

    def back_halo(pair):
        place = 2 * pair + jnp.where(pair < HALO // 2, 0, ROWS)
        both = jnp.concatenate([key_row(place), key_row(place + 1)], 1)
        ghalo[:, pl.ds(pl.multiple_of(pair * 16, 16), 16)] = both.astype(BF16)

    for_each(HALO, back_halo)

    def gnear_halo(rows):
        part = pl.ds(EDGE - rows * COLS, 2 * rows * COLS)
        down = send(
            ghalo.at[pl.ds(1, 3), part], chalo.at[1, :, part],
            gnear_send.at[0], gnear_recv.at[0], {"tm": tm - RING},
        )
        up = send(
            ghalo.at[pl.ds(12, 3), part], chalo.at[0, :, part],
            gnear_send.at[1], gnear_recv.at[1], {"tm": tm + RING},
        )
        return down, up

    def gnear_main():
        down = send(
            gmain.at[pl.ds(1, 3), 0], cmain.at[1], gnear_send.at[2], gnear_recv.at[2],
            {"tm": tm - RING},
        )
        up = send(
            gmain.at[pl.ds(12, 3), 0], cmain.at[0], gnear_send.at[3], gnear_recv.at[3],
            {"tm": tm + RING},
        )
        return down, up

    def gnear_halo_start(rows):
        pl.when(has_down)(lambda: gnear_halo(rows)[0].start())
        pl.when(has_up)(lambda: gnear_halo(rows)[1].start())

    by_group(gnear_halo_start)

    def back_main(pair):
        rows = pl.ds(pl.multiple_of(pair * 16, 16), 16)
        place = HALO + 2 * pair
        both = jnp.concatenate([key_row(place), key_row(place + 1)], 1)
        gmain[:, 0, rows] = both.astype(BF16)
        outs = [quers[2 * pair + i].astype(F32).reshape(RING, COLS, 2 * WIDTH) for i in range(2)]
        gmain[pl.ds(4, RING), 1, rows] = jnp.concatenate(outs, 1).astype(BF16)

    for_each(ROWS // 2, back_main)
    pl.when(has_down)(lambda: gnear_main()[0].start())
    pl.when(has_up)(lambda: gnear_main()[1].start())

    def ghalo_copies(rows, i):
        size = rows * COLS
        lower = pl.ds(EDGE - size, size)
        upper = pl.ds(EDGE, size)
        there = ring * RING + i
        downward = send(
            ghalo.at[i + 4, lower], rhalo.at[my_slot, lower], ghalo_send.at[i, 0],
            ghalo_recv.at[my_slot, 0], {"tm": there, "space": space - 1},
        )
        upward = send(
            ghalo.at[i + 4, upper], rhalo.at[my_slot, upper], ghalo_send.at[i, 1],
            ghalo_recv.at[my_slot, 1], {"tm": there, "space": space + 1},
        )
        return downward, upward

    def add_halo(rows):
        part = pl.ds(EDGE - rows * COLS, 2 * rows * COLS)

        def add(first, side):
            def one(i):
                both = ghalo[first + i, part].astype(F32) + chalo[side, i, part].astype(F32)
                ghalo[first + i, part] = both.astype(BF16)

            for_each(3, one)

        def start(i):
            pl.when(has_prev)(lambda: ghalo_copies(rows, i)[0].start())
            pl.when(has_next)(lambda: ghalo_copies(rows, i)[1].start())

        for_each(2, lambda i: start(i + 3))

        @pl.when(has_down)
        def _():
            gnear_halo(rows)[1].wait_recv()
            add(4, 0)

        for_each(3, start)

        @pl.when(has_up)
        def _():
            gnear_halo(rows)[0].wait_recv()
            add(9, 1)

        for_each(3, lambda i: start(i + 5))

    by_group(add_halo)

    def gmain_copies(i):
        at_home = send(
            gmain.at[i + 4], rmain.at[my_slot], gmain_send.at[i], gmain_recv.at[my_slot],
            {"tm": ring * RING + i},
        )
        local = pltpu.make_async_copy(gmain.at[i + 4], rmain.at[my_slot], gmain_recv.at[my_slot])
        return at_home, local

    def gmain_start(i):
        pl.when(i != me)(lambda: gmain_copies(i)[0].start())
        pl.when(i == me)(lambda: gmain_copies(i)[1].start())

    def add_main(first, side):
        def one(i):
            both = gmain[first + i, 0].astype(F32) + cmain[side, i].astype(F32)
            gmain[first + i, 0] = both.astype(BF16)

        for_each(3, one)

    for_each(2, lambda i: gmain_start(i + 3))

    @pl.when(has_down)
    def _():
        gnear_main()[1].wait_recv()
        add_main(4, 0)

    for_each(3, gmain_start)

    @pl.when(has_up)
    def _():
        gnear_main()[0].wait_recv()
        add_main(9, 1)

    for_each(3, lambda i: gmain_start(i + 5))

    for slot in range(HEADS):
        size = HALO_ROWS[slot] * COLS
        lower = pl.ds(EDGE - size, size)
        upper = pl.ds(EDGE, size)
        arrived(rmain.at[slot], gmain_recv.at[slot])
        final[...] = rmain[slot, 0].astype(F32)

        @pl.when(has_next)
        def _():
            arrived(rhalo.at[slot, lower], ghalo_recv.at[slot, 0])
            final[pl.ds(CELL - size, size)] += rhalo[slot, lower].astype(F32)

        @pl.when(has_prev)
        def _():
            arrived(rhalo.at[slot, upper], ghalo_recv.at[slot, 1])
            final[pl.ds(0, size)] += rhalo[slot, upper].astype(F32)

        result[slot, 0] = final[...].astype(BF16)
        result[slot, 1] = rmain[slot, 1]
        pltpu.make_async_copy(result.at[slot], output.at[slot], store.at[slot]).start()

    for slot in range(HEADS):
        upward, downward = halo_copies(slot)
        pl.when(has_next)(upward.wait_send)
        pl.when(has_prev)(downward.wait_send)

    def main_sent(slot):
        where, at_home, local = main_copies(slot)
        pl.when(where != me)(lambda: at_home.wait_send())

    for_each(HEADS, main_sent)

    def gmain_sent(i):
        pl.when(i != me)(lambda: gmain_copies(i)[0].wait_send())

    for_each(RING, gmain_sent)

    def edges_sent(rows):
        def one(i):
            pl.when(has_prev)(lambda: ghalo_copies(rows, i)[0].wait_send())
            pl.when(has_next)(lambda: ghalo_copies(rows, i)[1].wait_send())

        for_each(RING, one)
        for number, there in enumerate((has_down, has_up)):
            pl.when(there)(lambda: near_main()[number].wait_send())
            pl.when(there)(lambda: near_halo(rows)[number].wait_send())
            pl.when(there)(lambda: gnear_halo(rows)[number].wait_send())
            pl.when(there)(lambda: gnear_main()[number].wait_send())

    by_group(edges_sent)
    for slot in range(HEADS):
        pltpu.make_async_copy(result.at[slot], output.at[slot], store.at[slot]).wait()


def shards(queries, key_vectors, values, cotangent, dilation):
    frames, rows, cols, width = queries.shape
    flat = [a.reshape(CELL, width) for a in (queries, key_vectors, values, cotangent)]
    lanes = 2 * WIDTH
    dma = pltpu.SemaphoreType.DMA
    hbm = pl.BlockSpec(memory_space=pl.ANY)
    result = pl.pallas_call(
        functools.partial(main_kernel, lax.axis_size("tm") // RING, lax.axis_size("space")),
        out_shape=jax.ShapeDtypeStruct((HEADS, 2, CELL, lanes), BF16),
        in_specs=[hbm] * 5,
        out_specs=hbm,
        scratch_shapes=[
            pltpu.SMEM((HEADS,), jnp.int32),
        ]
        + [pltpu.VMEM((CELL, width), BF16)] * 4
        + [
            pltpu.VMEM((HEADS, 2, CELL, lanes), BF16),
            pltpu.VMEM((SPAN, 2, CELL, lanes), BF16),
            pltpu.VMEM((SPAN, 2 * EDGE, lanes), BF16),
            pltpu.VMEM((ROWS + 2 * HALO, SPAN * COLS, lanes), BF16),
            pltpu.VMEM((ROWS, RING * COLS, lanes), BF16),
            pltpu.VMEM((2, RING * COLS, SPAN * COLS), F32),
            pltpu.VMEM((4 * RING * COLS, 8 * SPAN * COLS), F32),
            pltpu.VMEM((4 * RING * COLS, 8 * SPAN * COLS), BF16),
            pltpu.VMEM((ROWS + 2 * HALO, lanes, SPAN * COLS), F32),
            pltpu.VMEM((SPAN, 2, CELL, lanes), BF16),
            pltpu.VMEM((SPAN, 2 * EDGE, lanes), BF16),
            pltpu.VMEM((2, REACH, CELL, lanes), BF16),
            pltpu.VMEM((2, REACH, 2 * EDGE, lanes), BF16),
            pltpu.VMEM((HEADS, 2, CELL, lanes), BF16),
            pltpu.VMEM((HEADS, 2 * EDGE, lanes), BF16),
            pltpu.VMEM((CELL, lanes), F32),
            pltpu.VMEM((HEADS, 2, CELL, lanes), BF16),
            dma((5,)),
            dma((HEADS,)),
            dma((HEADS,)),
            dma((RING,)),
            dma((HEADS, 2)),
            dma((RING, 2)),
            dma((4,)),
            dma((4,)),
            dma((RING,)),
            dma((HEADS,)),
            dma((RING, 2)),
            dma((HEADS, 2)),
            dma((4,)),
            dma((4,)),
        ],
        compiler_params=pltpu.CompilerParams(
            collective_id=0, has_side_effects=True, vmem_limit_bytes=56 * 1024 * 1024
        ),
        name="neighbourhood_attention",
    )(dilation, *flat)
    outs = pl.pallas_call(
        unpack_kernel,
        out_shape=[jax.ShapeDtypeStruct((CELL, width), BF16)] * 4,
        in_specs=[hbm] * 2,
        out_specs=[hbm] * 4,
        scratch_shapes=[
            pltpu.SMEM((HEADS,), jnp.int32),
            pltpu.VMEM((HEADS, 2, CELL, lanes), BF16),
        ]
        + [pltpu.VMEM((CELL, width), BF16)] * 4
        + [dma((HEADS + 1,)), dma((4,))],
        compiler_params=pltpu.CompilerParams(vmem_limit_bytes=56 * 1024 * 1024),
        name="unpack_heads",
    )(dilation, result)
    return tuple(a.reshape(frames, rows, cols, width) for a in outs)


def solution(mesh):
    placed = P("tm", "space", None, None)
    return jax.shard_map(
        shards,
        mesh=mesh,
        in_specs=(placed, placed, placed, placed, P()),
        out_specs=(placed, placed, placed, placed),
        check_vma=False,
    )
```

time: 75.3 us -> 68.3 us (0.907)
  the two profiles are of different devices: /device:TPU:89 before, /device:TPU:33 now
where the time goes in v2:
time: 68.3 us; the launch traced here: 68.1 us
  Pallas kernels  67.4 us (99%)
    pallas_call x1, Pallas kernels, shards(): pl.pallas_call(functools.partial(main_kernel, lax.axis_size('tm') // RING...  65.3 us
    pallas_call x1, Pallas kernels, shards(): pl.pallas_call(unpack_kernel, out_shape=[jax.ShapeDtypeStruct((CELL, widt...  2.13 us

profile of v2, /device:TPU:33, one launch (start us, length us, event | category | flops | bytes accessed | tf_op | source)
XLA Modules:
  0.0 68.1 jit_solution(13211232348298607882)
XLA Ops:
  0.6 65.3 %neighbourhood_attention.1.result_in = bf16[8,2,128,128]{3,2,1,0:T(8,128)(2,1)} custom-call(s32[8]{0:T(128)} %dilation_in.3, bf16[128,512]{1,0:T(8,128)(2,1)} %bitcast.8, bf16[128,512]{1,0:T(8,128)(2,1)} %bitcast.9, bf16[128,512]{1,0:T(8,128)(2,1)} %bitcast.10, bf16[128,512]{1,0:T(8,128)(2,1)} %bitcast.11), custom_call_target="tpu_custom_call" | custom-call | tf_op jit(solution)/shard_map/neighbourhood_attention/pallas_call | solution.py:669
  65.9 2.1 %unpack_heads.1 = (bf16[128,512]{1,0:T(8,128)(2,1)}, bf16[128,512]{1,0:T(8,128)(2,1)}, bf16[128,512]{1,0:T(8,128)(2,1)}, bf16[128,512]{1,0:T(8,128)(2,1)}) custom-call(s32[8]{0:T(128)} %dilation_in.3, bf16[8,2,128,128]{3,2,1,0:T(8,128)(2,1)} %neighbourhood_attention.1.result_in), custom_call_target="tpu_custom_call" | custom-call | tf_op jit(solution)/shard_map/unpack_heads/pallas_call | solution.py:716

commit v3 on v2

--- a/solution.py
+++ b/solution.py
@@ -23,6 +23,29 @@
 
 HALO_ROWS = (12, 12, 12, 12, 4, 4, 6, 6)
 GROUP_ROWS = (12, 4, 6)
+FAR = 4
+
+
+def own_place(pair, far):
+    return jnp.where(far, lax.rem(pair, 2) * 4 + lax.div(pair, 2), pair)
+
+
+def edge_place(pair, far):
+    return jnp.where(far, lax.rem(pair, 2) * 6 + lax.div(pair, 2), pair)
+
+
+def edge_parts(rows, half):
+    if rows == HALO:
+        return pl.ds(half * EDGE, EDGE // 2), pl.ds(half * EDGE + EDGE // 2, EDGE // 2), pl.ds(half * EDGE, EDGE)
+    size = rows * COLS
+    return pl.ds(EDGE - size, size), pl.ds(EDGE, size), pl.ds(EDGE - size, 2 * size)
+
+
+def own_parts(rows, half):
+    if rows == HALO:
+        return pl.ds(half * CELL // 2 + 16, EDGE // 2), pl.ds(half * CELL // 2, EDGE // 2)
+    size = rows * COLS
+    return pl.ds(CELL - size, size), pl.ds(0, size)
 
 
 def slot_device(slot):
@@ -65,7 +88,13 @@
         b = pick(second, chosen)
         a = jnp.where(odd, pltpu.roll(a, WIDTH, 1), a)
         b = jnp.where(odd, b, pltpu.roll(b, WIDTH, 1))
-        packed[slot, place] = jnp.where(low, a, b).astype(BF16)
+        block = jnp.where(low, a, b).astype(BF16)
+        if place == 0 and slot < FAR:
+            for pair in range(ROWS // 2):
+                target = ((pair % 2) * 4 + pair // 2) * 16
+                packed[slot, place, pl.ds(target, 16)] = block[pair * 16 : pair * 16 + 16]
+        else:
+            packed[slot, place] = block
 
 
 def unpack_kernel(
@@ -115,12 +144,13 @@
         copy.wait()
 
 
-def for_each(count, body):
+def for_each(count, body, unroll=1):
     def step(i, carry):
-        body(i)
+        for k in range(unroll):
+            body(i * unroll + k)
         return carry
 
-    lax.fori_loop(0, count, step, 0)
+    lax.fori_loop(0, count // unroll, step, 0)
 
 
 def main_kernel(
@@ -175,7 +205,8 @@
     me = lax.rem(tm, RING)
     my_slot = lax.rem(me, 2) * 4 + lax.div(me, 2)
     group = jnp.where(lax.rem(me, 2) == 0, 0, jnp.where(me < 4, 1, 2))
-    step = jnp.where(group == 0, 4, group)
+    far = group == 0
+    step = jnp.where(far, 4, group)
     has_down = ring > 0
     has_up = ring < rings - 1
     has_prev = space > 0
@@ -240,29 +271,33 @@
     )
     pl.semaphore_wait(barrier, greeted)
 
-    def halo_copies(slot):
-        size = HALO_ROWS[slot] * COLS
+    def halo_copies(slot, half):
+        top, bottom = own_parts(HALO_ROWS[slot], half)
+        lower, upper, _ = edge_parts(HALO_ROWS[slot], half)
         there = ring * RING + 2 * (slot % 4) + slot // 4
         upward = send(
-            packed.at[slot, 0, pl.ds(CELL - size, size)],
-            hstage.at[me + 4, pl.ds(EDGE - size, size)],
-            halo_send.at[slot, 0],
-            halo_recv.at[me, 0],
+            packed.at[slot, 0, top],
+            hstage.at[me + 4, lower],
+            halo_send.at[slot, 0, half],
+            halo_recv.at[me, 0, half],
             {"tm": there, "space": space + 1},
         )
         downward = send(
-            packed.at[slot, 0, pl.ds(0, size)],
-            hstage.at[me + 4, pl.ds(EDGE, size)],
-            halo_send.at[slot, 1],
-            halo_recv.at[me, 1],
+            packed.at[slot, 0, bottom],
+            hstage.at[me + 4, upper],
+            halo_send.at[slot, 1, half],
+            halo_recv.at[me, 1, half],
             {"tm": there, "space": space - 1},
         )
         return upward, downward
 
-    for slot in range(HEADS):
-        upward, downward = halo_copies(slot)
+    def halo_start(slot, half):
+        upward, downward = halo_copies(slot, half)
         pl.when(has_next)(upward.start)
         pl.when(has_prev)(downward.start)
+
+    for slot in (4, 5, 6, 7, 0, 1, 2, 3):
+        halo_start(slot, 0)
 
     for copy in loads[3:]:
         copy.wait()
@@ -296,14 +331,21 @@
     pl.when(jnp.logical_not(has_down))(lambda: clear(1, 3))
     pl.when(jnp.logical_not(has_up))(lambda: clear(12, 3))
 
-    def clear_halo(first):
+    def clear_halo(rows):
+        halves = range(2) if rows == HALO else range(1)
+
         def one(i):
-            hstage[i + 4, pl.ds(first, EDGE)] = jnp.zeros((EDGE, 2 * WIDTH), BF16)
+            for half in halves:
+                for number, missing in enumerate((has_prev, has_next)):
+                    part = edge_parts(rows, half)[number]
+
+                    @pl.when(jnp.logical_not(missing))
+                    def _():
+                        hstage[i + 4, part] = jnp.zeros((part.size, 2 * WIDTH), BF16)
 
         for_each(RING, one)
 
-    pl.when(jnp.logical_not(has_prev))(lambda: clear_halo(0))
-    pl.when(jnp.logical_not(has_next))(lambda: clear_halo(EDGE))
+    by_group(clear_halo)
 
     def clear_total(i):
         total[i] = jnp.zeros((2 * WIDTH, 2 * WIDTH), F32)
@@ -340,15 +382,15 @@
         )
         return down, up
 
-    def near_halo(rows):
-        part = pl.ds(EDGE - rows * COLS, 2 * rows * COLS)
+    def near_halo(rows, half):
+        part = edge_parts(rows, half)[2]
         down = send(
             hstage.at[pl.ds(4, 3), part], hstage.at[pl.ds(12, 3), part],
-            near_send.at[2], near_recv.at[2], {"tm": tm - RING},
+            near_send.at[2 + 2 * half], near_recv.at[2 + 2 * half], {"tm": tm - RING},
         )
         up = send(
             hstage.at[pl.ds(9, 3), part], hstage.at[pl.ds(1, 3), part],
-            near_send.at[3], near_recv.at[3], {"tm": tm + RING},
+            near_send.at[3 + 2 * half], near_recv.at[3 + 2 * half], {"tm": tm + RING},
         )
         return down, up
 
@@ -357,25 +399,24 @@
     for_each(3, lambda i: main_wait(i + 5))
     pl.when(has_up)(lambda: near_main()[1].start())
     for_each(2, lambda i: main_wait(i + 3))
-
-    def halo_phase(rows):
-        size = rows * COLS
+    for slot in range(FAR):
+        halo_start(slot, 1)
+
+
+    def halo_phase(half, rows):
+        lower, upper, _ = edge_parts(rows, half)
 
         def one(i):
-            pl.when(has_prev)(
-                lambda: arrived(hstage.at[i + 4, pl.ds(EDGE - size, size)], halo_recv.at[i, 0])
-            )
-            pl.when(has_next)(
-                lambda: arrived(hstage.at[i + 4, pl.ds(EDGE, size)], halo_recv.at[i, 1])
-            )
+            pl.when(has_prev)(lambda: arrived(hstage.at[i + 4, lower], halo_recv.at[i, 0, half]))
+            pl.when(has_next)(lambda: arrived(hstage.at[i + 4, upper], halo_recv.at[i, 1, half]))
 
         for_each(3, one)
-        pl.when(has_down)(lambda: near_halo(rows)[0].start())
+        pl.when(has_down)(lambda: near_halo(rows, half)[0].start())
         for_each(3, lambda i: one(i + 5))
-        pl.when(has_up)(lambda: near_halo(rows)[1].start())
+        pl.when(has_up)(lambda: near_halo(rows, half)[1].start())
         for_each(2, lambda i: one(i + 3))
 
-    by_group(halo_phase)
+    by_group(functools.partial(halo_phase, 0))
     pl.when(has_down)(lambda: near_main()[1].wait_recv())
     pl.when(has_up)(lambda: near_main()[0].wait_recv())
 
@@ -384,30 +425,31 @@
         return [wide[:, i].reshape(frames * COLS, 2 * WIDTH).astype(BF16) for i in range(2)]
 
     def turn_main(pair):
-        rows = pl.ds(pl.multiple_of(pair * 16, 16), 16)
-        even, odd = two_rows(main[:, 0, rows], SPAN)
+        place = pl.ds(pl.multiple_of(own_place(pair, far) * 16, 16), 16)
+        even, odd = two_rows(main[:, 0, place], SPAN)
         keys[HALO + 2 * pair] = even
         keys[HALO + 2 * pair + 1] = odd
+        rows = pl.ds(pl.multiple_of(pair * 16, 16), 16)
         even, odd = two_rows(main[pl.ds(4, RING), 1, rows], RING)
         quers[2 * pair] = even
         quers[2 * pair + 1] = odd
 
-    for_each(ROWS // 2, turn_main)
-
-    def near_halo_wait(rows):
-        pl.when(has_down)(lambda: near_halo(rows)[1].wait_recv())
-        pl.when(has_up)(lambda: near_halo(rows)[0].wait_recv())
-
-    by_group(near_halo_wait)
+    for_each(ROWS // 2, turn_main, 4)
+
+    def near_halo_wait(half, rows):
+        pl.when(has_down)(lambda: near_halo(rows, half)[1].wait_recv())
+        pl.when(has_up)(lambda: near_halo(rows, half)[0].wait_recv())
 
     def turn_halo(pair):
-        rows = pl.ds(pl.multiple_of(pair * 16, 16), 16)
+        rows = pl.ds(pl.multiple_of(edge_place(pair, far) * 16, 16), 16)
         even, odd = two_rows(hstage[:, rows], SPAN)
         place = 2 * pair + jnp.where(pair < HALO // 2, 0, ROWS)
         keys[place] = even
         keys[place + 1] = odd
 
-    for_each(HALO, turn_halo)
+    by_group(functools.partial(near_halo_wait, 0))
+    pl.when(far)(lambda: for_each(HALO // 2, lambda i: turn_halo(2 * i), 3))
+    pl.when(jnp.logical_not(far))(lambda: for_each(HALO, turn_halo, 3))
 
     low = low_lanes(RING * COLS)
     wide = SPAN * COLS
@@ -415,10 +457,10 @@
     scale = WIDTH ** -0.5 * 1.4426950408889634
     for part in range(4):
         unseen = pl.ds(0 if part % 2 else 7 * wide, wide)
-        probs[pl.ds(part * tall, tall), unseen] = jnp.zeros((tall, wide), BF16)
-
-    def attend(i):
-        first = lax.div(i, step) * (2 * step) + lax.rem(i, step)
+        for lane in range(2):
+            probs[lane, pl.ds(part * tall, tall), unseen] = jnp.zeros((tall, wide), BF16)
+
+    def score(lane, first):
         pair = [quers[first], quers[first + step]]
         none = jnp.zeros_like(pair[0])
         left = jnp.concatenate(
@@ -426,9 +468,12 @@
         )
         places = [first + HALO + step * (j - REACH) for j in range(8)]
         block = jnp.concatenate([keys[place] for place in places], 0)
-        scores[...] = lax.dot_general(
+        scores[lane] = lax.dot_general(
             left, block, (((1,), (1,)), ((), ())), preferred_element_type=F32
         )
+        return left, places, block
+
+    def soften(lane, places):
         outside = []
         for place in places:
             row = place - HALO + space * ROWS
@@ -440,13 +485,13 @@
                 grad_rows = pl.ds((2 + half) * tall + start, chunk)
                 tiles = range(half, half + 7)
                 raw = [
-                    scores[rows, pl.ds(j * wide, wide)]
+                    scores[lane, rows, pl.ds(j * wide, wide)]
                     + bias[outside[j], pl.ds(start, chunk)]
                     for j in tiles
                 ]
                 peak = jnp.max(functools.reduce(jnp.maximum, raw), axis=1, keepdims=True)
                 power = [jnp.exp2((tile - peak) * scale) for tile in raw]
-                gains = [scores[grad_rows, pl.ds(j * wide, wide)] for j in tiles]
+                gains = [scores[lane, grad_rows, pl.ds(j * wide, wide)] for j in tiles]
                 summed = jnp.sum(functools.reduce(jnp.add, power), axis=1, keepdims=True)
                 inverse = 1.0 / summed
                 delta = inverse * jnp.sum(
@@ -456,9 +501,11 @@
                 )
                 for j, a, b in zip(tiles, power, gains):
                     weight = a * inverse
-                    probs[grad_rows, pl.ds(j * wide, wide)] = weight.astype(BF16)
-                    probs[rows, pl.ds(j * wide, wide)] = (weight * (b - delta)).astype(BF16)
-        both = probs[...]
+                    probs[lane, grad_rows, pl.ds(j * wide, wide)] = weight.astype(BF16)
+                    probs[lane, rows, pl.ds(j * wide, wide)] = (weight * (b - delta)).astype(BF16)
+
+    def gather(lane, first, left, places, block):
+        both = probs[lane]
         out = jnp.dot(both, block, preferred_element_type=F32)
         for half in range(2):
             grad_query = out[half * tall : (half + 1) * tall] * WIDTH ** -0.5
@@ -468,7 +515,17 @@
         for j, place in enumerate(places):
             total[place] += back[:, j * wide : (j + 1) * wide]
 
-    for_each(ROWS // 2, attend)
+    def attend(turn):
+        firsts = []
+        for lane in range(2):
+            near = 2 * turn + lane
+            apart = lax.rem(turn, 2) * 4 + lane + 2 * lax.div(turn, 2)
+            i = jnp.where(far, apart, near)
+            firsts.append(lax.div(i, step) * (2 * step) + lax.rem(i, step))
+        scored = [score(lane, firsts[lane]) for lane in range(2)]
+        for lane in range(2):
+            soften(lane, scored[lane][1])
+            gather(lane, firsts[lane], *scored[lane])
 
     low_all = low_lanes(SPAN * COLS)
 
@@ -479,68 +536,62 @@
     def back_halo(pair):
         place = 2 * pair + jnp.where(pair < HALO // 2, 0, ROWS)
         both = jnp.concatenate([key_row(place), key_row(place + 1)], 1)
-        ghalo[:, pl.ds(pl.multiple_of(pair * 16, 16), 16)] = both.astype(BF16)
-
-    for_each(HALO, back_halo)
-
-    def gnear_halo(rows):
-        part = pl.ds(EDGE - rows * COLS, 2 * rows * COLS)
+        ghalo[:, pl.ds(pl.multiple_of(edge_place(pair, far) * 16, 16), 16)] = both.astype(BF16)
+
+    def gnear_halo(rows, half):
+        part = edge_parts(rows, half)[2]
         down = send(
             ghalo.at[pl.ds(1, 3), part], chalo.at[1, :, part],
-            gnear_send.at[0], gnear_recv.at[0], {"tm": tm - RING},
+            gnear_send.at[2 + 2 * half], gnear_recv.at[2 + 2 * half], {"tm": tm - RING},
         )
         up = send(
             ghalo.at[pl.ds(12, 3), part], chalo.at[0, :, part],
-            gnear_send.at[1], gnear_recv.at[1], {"tm": tm + RING},
+            gnear_send.at[3 + 2 * half], gnear_recv.at[3 + 2 * half], {"tm": tm + RING},
         )
         return down, up
 
     def gnear_main():
         down = send(
-            gmain.at[pl.ds(1, 3), 0], cmain.at[1], gnear_send.at[2], gnear_recv.at[2],
+            gmain.at[pl.ds(1, 3), 0], cmain.at[1], gnear_send.at[0], gnear_recv.at[0],
             {"tm": tm - RING},
         )
         up = send(
-            gmain.at[pl.ds(12, 3), 0], cmain.at[0], gnear_send.at[3], gnear_recv.at[3],
+            gmain.at[pl.ds(12, 3), 0], cmain.at[0], gnear_send.at[1], gnear_recv.at[1],
             {"tm": tm + RING},
         )
         return down, up
 
-    def gnear_halo_start(rows):
-        pl.when(has_down)(lambda: gnear_halo(rows)[0].start())
-        pl.when(has_up)(lambda: gnear_halo(rows)[1].start())
-
-    by_group(gnear_halo_start)
+    def gnear_start(half, rows):
+        pl.when(has_down)(lambda: gnear_halo(rows, half)[0].start())
+        pl.when(has_up)(lambda: gnear_halo(rows, half)[1].start())
 
     def back_main(pair):
         rows = pl.ds(pl.multiple_of(pair * 16, 16), 16)
         place = HALO + 2 * pair
         both = jnp.concatenate([key_row(place), key_row(place + 1)], 1)
-        gmain[:, 0, rows] = both.astype(BF16)
+        gmain[:, 0, pl.ds(pl.multiple_of(own_place(pair, far) * 16, 16), 16)] = both.astype(BF16)
         outs = [quers[2 * pair + i].astype(F32).reshape(RING, COLS, 2 * WIDTH) for i in range(2)]
         gmain[pl.ds(4, RING), 1, rows] = jnp.concatenate(outs, 1).astype(BF16)
 
-    for_each(ROWS // 2, back_main)
-    pl.when(has_down)(lambda: gnear_main()[0].start())
-    pl.when(has_up)(lambda: gnear_main()[1].start())
-
-    def ghalo_copies(rows, i):
-        size = rows * COLS
-        lower = pl.ds(EDGE - size, size)
-        upper = pl.ds(EDGE, size)
+    def ghalo_copies(rows, half, i):
+        lower, upper, _ = edge_parts(rows, half)
         there = ring * RING + i
         downward = send(
-            ghalo.at[i + 4, lower], rhalo.at[my_slot, lower], ghalo_send.at[i, 0],
-            ghalo_recv.at[my_slot, 0], {"tm": there, "space": space - 1},
+            ghalo.at[i + 4, lower], rhalo.at[my_slot, lower], ghalo_send.at[i, 0, half],
+            ghalo_recv.at[my_slot, 0, half], {"tm": there, "space": space - 1},
         )
         upward = send(
-            ghalo.at[i + 4, upper], rhalo.at[my_slot, upper], ghalo_send.at[i, 1],
-            ghalo_recv.at[my_slot, 1], {"tm": there, "space": space + 1},
+            ghalo.at[i + 4, upper], rhalo.at[my_slot, upper], ghalo_send.at[i, 1, half],
+            ghalo_recv.at[my_slot, 1, half], {"tm": there, "space": space + 1},
         )
         return downward, upward
 
-    def add_halo(rows):
-        part = pl.ds(EDGE - rows * COLS, 2 * rows * COLS)
+    def ghalo_start(half, rows, i):
+        pl.when(has_prev)(lambda: ghalo_copies(rows, half, i)[0].start())
+        pl.when(has_next)(lambda: ghalo_copies(rows, half, i)[1].start())
+
+    def add_halo(half, rows):
+        part = edge_parts(rows, half)[2]
 
         def add(first, side):
             def one(i):
@@ -549,27 +600,52 @@
 
             for_each(3, one)
 
-        def start(i):
-            pl.when(has_prev)(lambda: ghalo_copies(rows, i)[0].start())
-            pl.when(has_next)(lambda: ghalo_copies(rows, i)[1].start())
-
-        for_each(2, lambda i: start(i + 3))
+        for_each(2, lambda i: ghalo_start(half, rows, i + 3))
 
         @pl.when(has_down)
         def _():
-            gnear_halo(rows)[1].wait_recv()
+            gnear_halo(rows, half)[1].wait_recv()
             add(4, 0)
 
-        for_each(3, start)
+        for_each(3, lambda i: ghalo_start(half, rows, i))
 
         @pl.when(has_up)
         def _():
-            gnear_halo(rows)[0].wait_recv()
+            gnear_halo(rows, half)[0].wait_recv()
             add(9, 1)
 
-        for_each(3, lambda i: start(i + 5))
-
-    by_group(add_halo)
+        for_each(3, lambda i: ghalo_start(half, rows, i + 5))
+
+    def advance(turn):
+        @pl.when(far & (turn == 2))
+        def _():
+            near_halo_wait(1, HALO)
+            for_each(HALO // 2, lambda i: turn_halo(2 * i + 1), 3)
+
+        attend(turn)
+
+        @pl.when(far & (turn == 0))
+        def _():
+            halo_phase(1, HALO)
+
+        @pl.when(far & (turn == 1))
+        def _():
+            for_each(HALO // 2, lambda i: back_halo(2 * i), 3)
+            gnear_start(0, HALO)
+
+        @pl.when(far & (turn == 2))
+        def _():
+            add_halo(0, HALO)
+
+    for_each(4, advance)
+
+    pl.when(far)(lambda: for_each(HALO // 2, lambda i: back_halo(2 * i + 1), 3))
+    pl.when(jnp.logical_not(far))(lambda: for_each(HALO, back_halo, 3))
+    by_group(functools.partial(gnear_start, 1))
+    for_each(ROWS // 2, back_main, 4)
+    pl.when(has_down)(lambda: gnear_main()[0].start())
+    pl.when(has_up)(lambda: gnear_main()[1].start())
+    by_group(functools.partial(add_halo, 1))
 
     def gmain_copies(i):
         at_home = send(
@@ -606,31 +682,43 @@
 
     for_each(3, lambda i: gmain_start(i + 5))
 
-    for slot in range(HEADS):
-        size = HALO_ROWS[slot] * COLS
-        lower = pl.ds(EDGE - size, size)
-        upper = pl.ds(EDGE, size)
+    for slot in (4, 5, 6, 7, 0, 1, 2, 3):
+        rows = HALO_ROWS[slot]
         arrived(rmain.at[slot], gmain_recv.at[slot])
-        final[...] = rmain[slot, 0].astype(F32)
-
-        @pl.when(has_next)
-        def _():
-            arrived(rhalo.at[slot, lower], ghalo_recv.at[slot, 0])
-            final[pl.ds(CELL - size, size)] += rhalo[slot, lower].astype(F32)
-
-        @pl.when(has_prev)
-        def _():
-            arrived(rhalo.at[slot, upper], ghalo_recv.at[slot, 1])
-            final[pl.ds(0, size)] += rhalo[slot, upper].astype(F32)
+        if slot < FAR:
+            for pair in range(ROWS // 2):
+                source = ((pair % 2) * 4 + pair // 2) * 16
+                final[pl.ds(pair * 16, 16)] = rmain[slot, 0, pl.ds(source, 16)].astype(F32)
+        else:
+            final[...] = rmain[slot, 0].astype(F32)
+        for number, there in enumerate((has_next, has_prev)):
+
+            @pl.when(there)
+            def _():
+                for half in range(2) if slot < FAR else (1,):
+                    arrived(
+                        rhalo.at[slot, edge_parts(rows, half)[number]],
+                        ghalo_recv.at[slot, number, half],
+                    )
+                for pair in range(rows // 2):
+                    if slot < FAR:
+                        source = (pair % 2) * 6 + pair // 2 + 3 * number
+                    else:
+                        source = 6 + pair - (0 if number else rows // 2)
+                    target = pair if number else ROWS // 2 - rows // 2 + pair
+                    final[pl.ds(target * 16, 16)] += rhalo[
+                        slot, pl.ds(source * 16, 16)
+                    ].astype(F32)
 
         result[slot, 0] = final[...].astype(BF16)
         result[slot, 1] = rmain[slot, 1]
         pltpu.make_async_copy(result.at[slot], output.at[slot], store.at[slot]).start()
 
     for slot in range(HEADS):
-        upward, downward = halo_copies(slot)
-        pl.when(has_next)(upward.wait_send)
-        pl.when(has_prev)(downward.wait_send)
+        for half in range(2) if slot < FAR else (0,):
+            upward, downward = halo_copies(slot, half)
+            pl.when(has_next)(upward.wait_send)
+            pl.when(has_prev)(downward.wait_send)
 
     def main_sent(slot):
         where, at_home, local = main_copies(slot)
@@ -645,15 +733,18 @@
 
     def edges_sent(rows):
         def one(i):
-            pl.when(has_prev)(lambda: ghalo_copies(rows, i)[0].wait_send())
-            pl.when(has_next)(lambda: ghalo_copies(rows, i)[1].wait_send())
+            for half in range(2) if rows == HALO else (1,):
+                pl.when(has_prev)(lambda: ghalo_copies(rows, half, i)[0].wait_send())
+                pl.when(has_next)(lambda: ghalo_copies(rows, half, i)[1].wait_send())
 
         for_each(RING, one)
         for number, there in enumerate((has_down, has_up)):
             pl.when(there)(lambda: near_main()[number].wait_send())
-            pl.when(there)(lambda: near_halo(rows)[number].wait_send())
-            pl.when(there)(lambda: gnear_halo(rows)[number].wait_send())
             pl.when(there)(lambda: gnear_main()[number].wait_send())
+            for half in range(2) if rows == HALO else (0,):
+                pl.when(there)(lambda: near_halo(rows, half)[number].wait_send())
+            for half in range(2) if rows == HALO else (1,):
+                pl.when(there)(lambda: gnear_halo(rows, half)[number].wait_send())
 
     by_group(edges_sent)
     for slot in range(HEADS):
@@ -682,8 +773,8 @@
             pltpu.VMEM((ROWS + 2 * HALO, SPAN * COLS, lanes), BF16),
             pltpu.VMEM((ROWS, RING * COLS, lanes), BF16),
             pltpu.VMEM((2, RING * COLS, SPAN * COLS), F32),
-            pltpu.VMEM((4 * RING * COLS, 8 * SPAN * COLS), F32),
-            pltpu.VMEM((4 * RING * COLS, 8 * SPAN * COLS), BF16),
+            pltpu.VMEM((2, 4 * RING * COLS, 8 * SPAN * COLS), F32),
+            pltpu.VMEM((2, 4 * RING * COLS, 8 * SPAN * COLS), BF16),
             pltpu.VMEM((ROWS + 2 * HALO, lanes, SPAN * COLS), F32),
             pltpu.VMEM((SPAN, 2, CELL, lanes), BF16),
             pltpu.VMEM((SPAN, 2 * EDGE, lanes), BF16),
@@ -697,16 +788,16 @@
             dma((HEADS,)),
             dma((HEADS,)),
             dma((RING,)),
-            dma((HEADS, 2)),
-            dma((RING, 2)),
-            dma((4,)),
-            dma((4,)),
+            dma((HEADS, 2, 2)),
+            dma((RING, 2, 2)),
+            dma((6,)),
+            dma((6,)),
             dma((RING,)),
             dma((HEADS,)),
-            dma((RING, 2)),
-            dma((HEADS, 2)),
-            dma((4,)),
-            dma((4,)),
+            dma((RING, 2, 2)),
+            dma((HEADS, 2, 2)),
+            dma((6,)),
+            dma((6,)),
         ],
         compiler_params=pltpu.CompilerParams(
             collective_id=0, has_side_effects=True, vmem_limit_bytes=56 * 1024 * 1024

time: 68.3 us -> 64 us (0.937)
  the two profiles are of different devices: /device:TPU:33 before, /device:TPU:17 now
where the time goes in v3:
time: 64 us; the launch traced here: 63.8 us
  Pallas kernels  63.1 us (99%)
  between operations  0.64 us (1%)
    pallas_call x1, Pallas kernels, shards(): pl.pallas_call(functools.partial(main_kernel, lax.axis_size('tm') // RING...  61 us
    pallas_call x1, Pallas kernels, shards(): pl.pallas_call(unpack_kernel, out_shape=[jax.ShapeDtypeStruct((CELL, widt...  2.13 us

profile of v3, /device:TPU:17, one launch (start us, length us, event | category | flops | bytes accessed | tf_op | source)
XLA Modules:
  0.0 63.8 jit_solution(2300139708084944189)
XLA Ops:
  0.6 61.0 %neighbourhood_attention.1.result_in = bf16[8,2,128,128]{3,2,1,0:T(8,128)(2,1)} custom-call(s32[8]{0:T(128)} %dilation_in.3, bf16[128,512]{1,0:T(8,128)(2,1)} %bitcast.8, bf16[128,512]{1,0:T(8,128)(2,1)} %bitcast.9, bf16[128,512]{1,0:T(8,128)(2,1)} %bitcast.10, bf16[128,512]{1,0:T(8,128)(2,1)} %bitcast.11), custom_call_target="tpu_custom_call" | custom-call | tf_op jit(solution)/shard_map/neighbourhood_attention/pallas_call | solution.py:760
  61.6 2.1 %unpack_heads.1 = (bf16[128,512]{1,0:T(8,128)(2,1)}, bf16[128,512]{1,0:T(8,128)(2,1)}, bf16[128,512]{1,0:T(8,128)(2,1)}, bf16[128,512]{1,0:T(8,128)(2,1)}) custom-call(s32[8]{0:T(128)} %dilation_in.3, bf16[8,2,128,128]{3,2,1,0:T(8,128)(2,1)} %neighbourhood_attention.1.result_in), custom_call_target="tpu_custom_call" | custom-call | tf_op jit(solution)/shard_map/unpack_heads/pallas_call | solution.py:807

commit v4 on v3

--- a/solution.py
+++ b/solution.py
@@ -24,6 +24,7 @@
 HALO_ROWS = (12, 12, 12, 12, 4, 4, 6, 6)
 GROUP_ROWS = (12, 4, 6)
 FAR = 4
+LANES = 4
 
 
 def own_place(pair, far):
@@ -249,13 +250,18 @@
     def hello(where):
         pl.semaphore_signal(barrier, inc=1, device_id=where, device_id_type=MESH)
 
-    def greet(i):
-        there = ring * RING + i
-        pl.when(i != me)(lambda: hello({"tm": there}))
-        pl.when(has_prev)(lambda: hello({"tm": there, "space": space - 1}))
-        pl.when(has_next)(lambda: hello({"tm": there, "space": space + 1}))
-
-    for_each(RING, greet)
+    @pl.when(has_next)
+    def _():
+        for i in range(RING):
+            hello({"tm": ring * RING + i, "space": space + 1})
+
+    @pl.when(has_prev)
+    def _():
+        for i in range(RING):
+            hello({"tm": ring * RING + i, "space": space - 1})
+
+    for i in range(1, RING):
+        hello({"tm": ring * RING + lax.rem(me + i, RING)})
     pl.when(has_down)(lambda: hello({"tm": tm - RING}))
     pl.when(has_up)(lambda: hello({"tm": tm + RING}))
     for copy in loads[:3]:
@@ -299,25 +305,27 @@
     for slot in (4, 5, 6, 7, 0, 1, 2, 3):
         halo_start(slot, 0)
 
+    def main_copies(slot, place):
+        where = slot_device(slot)
+        source = packed.at[slot, place]
+        target = main.at[me + 4, place]
+        arrival = main_recv.at[me, place]
+        at_home = send(
+            source, target, main_send.at[slot, place], arrival, {"tm": ring * RING + where}
+        )
+        local = pltpu.make_async_copy(source, target, arrival)
+        return where, at_home, local
+
+    def main_start(slot, place):
+        where, at_home, local = main_copies(slot, place)
+        pl.when(where != me)(lambda: at_home.start())
+        pl.when(where == me)(lambda: local.start())
+
+    for_each(HEADS, lambda slot: main_start(slot, 0))
     for copy in loads[3:]:
         copy.wait()
     pack(dilation, query, grad, packed, 1)
-
-    def main_copies(slot):
-        where = slot_device(slot)
-        at_home = send(
-            packed.at[slot], main.at[me + 4], main_send.at[slot], main_recv.at[me],
-            {"tm": ring * RING + where},
-        )
-        local = pltpu.make_async_copy(packed.at[slot], main.at[me + 4], main_recv.at[me])
-        return where, at_home, local
-
-    def main_start(slot):
-        where, at_home, local = main_copies(slot)
-        pl.when(where != me)(lambda: at_home.start())
-        pl.when(where == me)(lambda: local.start())
-
-    for_each(HEADS, main_start)
+    for_each(HEADS, lambda slot: main_start(slot, 1))
 
     def clear(first, count):
         def one(i):
@@ -369,7 +377,7 @@
     bias[1] = jnp.full(shape, -1e30, F32)
 
     def main_wait(i):
-        arrived(main.at[i + 4], main_recv.at[i])
+        arrived(main.at[i + 4, 0], main_recv.at[i, 0])
 
     def near_main():
         down = send(
@@ -434,6 +442,7 @@
         quers[2 * pair] = even
         quers[2 * pair + 1] = odd
 
+    for_each(RING, lambda i: arrived(main.at[i + 4, 1], main_recv.at[i, 1]))
     for_each(ROWS // 2, turn_main, 4)
 
     def near_halo_wait(half, rows):
@@ -450,6 +459,7 @@
     by_group(functools.partial(near_halo_wait, 0))
     pl.when(far)(lambda: for_each(HALO // 2, lambda i: turn_halo(2 * i), 3))
     pl.when(jnp.logical_not(far))(lambda: for_each(HALO, turn_halo, 3))
+    pl.when(far)(lambda: halo_phase(1, HALO))
 
     low = low_lanes(RING * COLS)
     wide = SPAN * COLS
@@ -457,7 +467,7 @@
     scale = WIDTH ** -0.5 * 1.4426950408889634
     for part in range(4):
         unseen = pl.ds(0 if part % 2 else 7 * wide, wide)
-        for lane in range(2):
+        for lane in range(LANES):
             probs[lane, pl.ds(part * tall, tall), unseen] = jnp.zeros((tall, wide), BF16)
 
     def score(lane, first):
@@ -517,13 +527,13 @@
 
     def attend(turn):
         firsts = []
-        for lane in range(2):
-            near = 2 * turn + lane
-            apart = lax.rem(turn, 2) * 4 + lane + 2 * lax.div(turn, 2)
+        for lane in range(LANES):
+            near = LANES * turn + lane
+            apart = (lane // 2) * 4 + lane % 2 + 2 * turn
             i = jnp.where(far, apart, near)
             firsts.append(lax.div(i, step) * (2 * step) + lax.rem(i, step))
-        scored = [score(lane, firsts[lane]) for lane in range(2)]
-        for lane in range(2):
+        scored = [score(lane, firsts[lane]) for lane in range(LANES)]
+        for lane in range(LANES):
             soften(lane, scored[lane][1])
             gather(lane, firsts[lane], *scored[lane])
 
@@ -617,7 +627,7 @@
         for_each(3, lambda i: ghalo_start(half, rows, i + 5))
 
     def advance(turn):
-        @pl.when(far & (turn == 2))
+        @pl.when(far & (turn == 1))
         def _():
             near_halo_wait(1, HALO)
             for_each(HALO // 2, lambda i: turn_halo(2 * i + 1), 3)
@@ -626,22 +636,15 @@
 
         @pl.when(far & (turn == 0))
         def _():
-            halo_phase(1, HALO)
-
-        @pl.when(far & (turn == 1))
-        def _():
             for_each(HALO // 2, lambda i: back_halo(2 * i), 3)
             gnear_start(0, HALO)
 
-        @pl.when(far & (turn == 2))
-        def _():
-            add_halo(0, HALO)
-
-    for_each(4, advance)
+    for_each(2, advance)
 
     pl.when(far)(lambda: for_each(HALO // 2, lambda i: back_halo(2 * i + 1), 3))
     pl.when(jnp.logical_not(far))(lambda: for_each(HALO, back_halo, 3))
     by_group(functools.partial(gnear_start, 1))
+    pl.when(far)(lambda: add_halo(0, HALO))
     for_each(ROWS // 2, back_main, 4)
     pl.when(has_down)(lambda: gnear_main()[0].start())
     pl.when(has_up)(lambda: gnear_main()[1].start())
@@ -721,8 +724,9 @@
             pl.when(has_prev)(downward.wait_send)
 
     def main_sent(slot):
-        where, at_home, local = main_copies(slot)
-        pl.when(where != me)(lambda: at_home.wait_send())
+        for place in range(2):
+            where, at_home, local = main_copies(slot, place)
+            pl.when(where != me)(lambda: at_home.wait_send())
 
     for_each(HEADS, main_sent)
 
@@ -773,8 +777,8 @@
             pltpu.VMEM((ROWS + 2 * HALO, SPAN * COLS, lanes), BF16),
             pltpu.VMEM((ROWS, RING * COLS, lanes), BF16),
             pltpu.VMEM((2, RING * COLS, SPAN * COLS), F32),
-            pltpu.VMEM((2, 4 * RING * COLS, 8 * SPAN * COLS), F32),
-            pltpu.VMEM((2, 4 * RING * COLS, 8 * SPAN * COLS), BF16),
+            pltpu.VMEM((LANES, 4 * RING * COLS, 8 * SPAN * COLS), F32),
+            pltpu.VMEM((LANES, 4 * RING * COLS, 8 * SPAN * COLS), BF16),
             pltpu.VMEM((ROWS + 2 * HALO, lanes, SPAN * COLS), F32),
             pltpu.VMEM((SPAN, 2, CELL, lanes), BF16),
             pltpu.VMEM((SPAN, 2 * EDGE, lanes), BF16),
@@ -786,8 +790,8 @@
             pltpu.VMEM((HEADS, 2, CELL, lanes), BF16),
             dma((5,)),
             dma((HEADS,)),
-            dma((HEADS,)),
-            dma((RING,)),
+            dma((HEADS, 2)),
+            dma((RING, 2)),
             dma((HEADS, 2, 2)),
             dma((RING, 2, 2)),
             dma((6,)),

time: 64 us -> 63.1 us (0.986)
  the two profiles are of different devices: /device:TPU:17 before, /device:TPU:41 now
where the time goes in v4:
time: 63.1 us; the launch traced here: 62.9 us
  Pallas kernels  62.3 us (99%)
  between operations  0.64 us (1%)
    pallas_call x1, Pallas kernels, shards(): pl.pallas_call(functools.partial(main_kernel, lax.axis_size('tm') // RING...  60.2 us
    pallas_call x1, Pallas kernels, shards(): pl.pallas_call(unpack_kernel, out_shape=[jax.ShapeDtypeStruct((CELL, widt...  2.13 us

profile of v4, /device:TPU:41, one launch (start us, length us, event | category | flops | bytes accessed | tf_op | source)
XLA Modules:
  0.0 62.9 jit_solution(8795106983209442311)
XLA Ops:
  0.6 60.2 %neighbourhood_attention.1.result_in = bf16[8,2,128,128]{3,2,1,0:T(8,128)(2,1)} custom-call(s32[8]{0:T(128)} %dilation_in.3, bf16[128,512]{1,0:T(8,128)(2,1)} %bitcast.8, bf16[128,512]{1,0:T(8,128)(2,1)} %bitcast.9, bf16[128,512]{1,0:T(8,128)(2,1)} %bitcast.10, bf16[128,512]{1,0:T(8,128)(2,1)} %bitcast.11), custom_call_target="tpu_custom_call" | custom-call | tf_op jit(solution)/shard_map/neighbourhood_attention/pallas_call | solution.py:764
  60.8 2.1 %unpack_heads.1 = (bf16[128,512]{1,0:T(8,128)(2,1)}, bf16[128,512]{1,0:T(8,128)(2,1)}, bf16[128,512]{1,0:T(8,128)(2,1)}, bf16[128,512]{1,0:T(8,128)(2,1)}) custom-call(s32[8]{0:T(128)} %dilation_in.3, bf16[8,2,128,128]{3,2,1,0:T(8,128)(2,1)} %neighbourhood_attention.1.result_in), custom_call_target="tpu_custom_call" | custom-call | tf_op jit(solution)/shard_map/unpack_heads/pallas_call | solution.py:811

commit v5 on v4

--- a/solution.py
+++ b/solution.py
@@ -114,21 +114,29 @@
     load,
     store,
 ):
+    order = pltpu.make_async_copy(dilation_in, dilation, load.at[2 * HEADS])
+    order.start()
     loads = [
-        pltpu.make_async_copy(result_in.at[slot], result.at[slot], load.at[slot])
-        for slot in range(HEADS)
+        [
+            pltpu.make_async_copy(
+                result_in.at[slot, place], result.at[slot, place], load.at[place * HEADS + slot]
+            )
+            for slot in range(HEADS)
+        ]
+        for place in range(2)
     ]
-    loads.append(pltpu.make_async_copy(dilation_in, dilation, load.at[HEADS]))
-    for copy in loads:
-        copy.start()
-    for copy in loads:
-        copy.wait()
+    for place in (1, 0):
+        for copy in loads[place]:
+            copy.start()
+    order.wait()
     ranks = head_ranks(dilation)
     low = low_lanes(CELL)
     pairs = ((grad_key, grad_value), (grad_query, attended))
     outs = ((grad_key_out, grad_value_out), (grad_query_out, attended_out))
     stores = []
-    for place in range(2):
+    for place in (1, 0):
+        for copy in loads[place]:
+            copy.wait()
         first, second = pairs[place]
         for block in range(HEADS // 2):
             slots = [lax.rem(ranks[2 * block + i] + 4, HEADS) for i in range(2)]
@@ -688,6 +696,7 @@
     for slot in (4, 5, 6, 7, 0, 1, 2, 3):
         rows = HALO_ROWS[slot]
         arrived(rmain.at[slot], gmain_recv.at[slot])
+        pltpu.make_async_copy(rmain.at[slot, 1], output.at[slot, 1], store.at[HEADS + slot]).start()
         if slot < FAR:
             for pair in range(ROWS // 2):
                 source = ((pair % 2) * 4 + pair // 2) * 16
@@ -714,8 +723,7 @@
                     ].astype(F32)
 
         result[slot, 0] = final[...].astype(BF16)
-        result[slot, 1] = rmain[slot, 1]
-        pltpu.make_async_copy(result.at[slot], output.at[slot], store.at[slot]).start()
+        pltpu.make_async_copy(result.at[slot, 0], output.at[slot, 0], store.at[slot]).start()
 
     for slot in range(HEADS):
         for half in range(2) if slot < FAR else (0,):
@@ -752,7 +760,8 @@
 
     by_group(edges_sent)
     for slot in range(HEADS):
-        pltpu.make_async_copy(result.at[slot], output.at[slot], store.at[slot]).wait()
+        pltpu.make_async_copy(result.at[slot, 0], output.at[slot, 0], store.at[slot]).wait()
+        pltpu.make_async_copy(rmain.at[slot, 1], output.at[slot, 1], store.at[HEADS + slot]).wait()
 
 
 def shards(queries, key_vectors, values, cotangent, dilation):
@@ -789,7 +798,7 @@
             pltpu.VMEM((CELL, lanes), F32),
             pltpu.VMEM((HEADS, 2, CELL, lanes), BF16),
             dma((5,)),
-            dma((HEADS,)),
+            dma((2 * HEADS,)),
             dma((HEADS, 2)),
             dma((RING, 2)),
             dma((HEADS, 2, 2)),
@@ -818,7 +827,7 @@
             pltpu.VMEM((HEADS, 2, CELL, lanes), BF16),
         ]
         + [pltpu.VMEM((CELL, width), BF16)] * 4
-        + [dma((HEADS + 1,)), dma((4,))],
+        + [dma((2 * HEADS + 1,)), dma((4,))],
         compiler_params=pltpu.CompilerParams(vmem_limit_bytes=56 * 1024 * 1024),
         name="unpack_heads",
     )(dilation, result)

time: 63.1 us -> 63.1 us (level)
  no operation moved by 1% of the time
where the time goes in v5:
time: 63.1 us; the launch traced here: 62.9 us
  Pallas kernels  62.3 us (99%)
  between operations  0.64 us (1%)
    pallas_call x1, Pallas kernels, shards(): pl.pallas_call(functools.partial(main_kernel, lax.axis_size('tm') // RING...  60.2 us
    pallas_call x1, Pallas kernels, shards(): pl.pallas_call(unpack_kernel, out_shape=[jax.ShapeDtypeStruct((CELL, widt...  2.04 us

profile of v5, /device:TPU:41, one launch (start us, length us, event | category | flops | bytes accessed | tf_op | source)
XLA Modules:
  0.0 62.9 jit_solution(2734524340149288061)
XLA Ops:
  0.6 60.2 %neighbourhood_attention.1.result_in = bf16[8,2,128,128]{3,2,1,0:T(8,128)(2,1)} custom-call(s32[8]{0:T(128)} %dilation_in.3, bf16[128,512]{1,0:T(8,128)(2,1)} %bitcast.8, bf16[128,512]{1,0:T(8,128)(2,1)} %bitcast.9, bf16[128,512]{1,0:T(8,128)(2,1)} %bitcast.10, bf16[128,512]{1,0:T(8,128)(2,1)} %bitcast.11), custom_call_target="tpu_custom_call" | custom-call | tf_op jit(solution)/shard_map/neighbourhood_attention/pallas_call | solution.py:773
  60.9 2.0 %unpack_heads.1 = (bf16[128,512]{1,0:T(8,128)(2,1)}, bf16[128,512]{1,0:T(8,128)(2,1)}, bf16[128,512]{1,0:T(8,128)(2,1)}, bf16[128,512]{1,0:T(8,128)(2,1)}) custom-call(s32[8]{0:T(128)} %dilation_in.3, bf16[8,2,128,128]{3,2,1,0:T(8,128)(2,1)} %neighbourhood_attention.1.result_in), custom_call_target="tpu_custom_call" | custom-call | tf_op jit(solution)/shard_map/unpack_heads/pallas_call | solution.py:820
